TPU v7x, 32 devices: a whole 2x2x4 slice. The times are simulated.
32 devices in a mesh: seq: 16 (over z, x, core), fsdp: 2 (over y).
Axes of the slice: x: 2, y: 2, z: 4, core: 2. Of those that a mesh axis runs over, the one named last changes fastest.
Arguments:
- block_input: bfloat16 [8, 8192, 768], P('fsdp', 'seq'), may hold values from -6 to 6
- gain_before: bfloat16 [768], P(('seq', 'fsdp')), may hold values from 0.5 to 1.5
- joint_weight: bfloat16 [768, 2304], P(('seq', 'fsdp')), may hold values from -0.21875 to 0.21875
- mixing_weight: bfloat16 [768, 768], P(('seq', 'fsdp')), may hold values from -1.25 to 1.25
- gain_middle: bfloat16 [768], P(('seq', 'fsdp')), may hold values from 0.5 to 1.5
- expand_weight: bfloat16 [768, 2304], P(('seq', 'fsdp')), may hold values from -0.21875 to 0.21875
- reduce_weight: bfloat16 [1152, 768], P(None, ('seq', 'fsdp')), may hold values from -0.25 to 0.25
- upstream: bfloat16 [8, 8192, 768], P('fsdp', 'seq'), may hold values from -8 to 8
Outputs:
- block_output: bfloat16 [8, 8192, 768], P('fsdp', 'seq')
- input_grad: float32 [8, 8192, 768], P('fsdp', 'seq')
- before_grad: float32 [768], P(('seq', 'fsdp'))
- joint_grad: float32 [768, 2304], P(('seq', 'fsdp'))
- mixing_grad: float32 [768, 768], P(('seq', 'fsdp'))
- middle_grad: float32 [768], P(('seq', 'fsdp'))
- expand_grad: float32 [768, 2304], P(('seq', 'fsdp'))
- reduce_grad: float32 [1152, 768], P(None, ('seq', 'fsdp'))
All inputs are finite; a program needn't handle non-finite values.
Results may differ from a plain program's by a relative error of at most 0.015.
Values may be sent and summed in bfloat16 or wider, within the bound.
A program may use at most 256 MiB of HBM per device.

v0:
```python
import math

import jax
import jax.numpy as jnp
from jax import lax
from jax.sharding import PartitionSpec as P

D = 768
HEADS = 12
HEAD_DIM = 64
FF = 1152
REACH = 64
PIECE = 512
GROUP_SEQS = 4


epsilon = 1e-05
masked_value = -1e30


def with_halo(cells, sides, width):
    for axis, dim in sides:
        count = lax.axis_size(axis)
        ends = count - 1
        head = lax.slice_in_dim(cells, 0, width, axis=dim)
        tail = lax.slice_in_dim(cells, cells.shape[dim] - width, cells.shape[dim], axis=dim)
        cells = jnp.concatenate(
            [
                lax.ppermute(tail, axis, [(i, (i + 1) % count) for i in range(ends)]),
                cells,
                lax.ppermute(head, axis, [((i + 1) % count, i) for i in range(ends)]),
            ],
            axis=dim,
        )
    return cells


def passed_along(x, axis, by):
    devices = lax.axis_size(axis)
    pairs = [(i, i + by) for i in range(devices) if 0 <= i + by < devices]
    return lax.ppermute(x, axis, pairs)


def layer_norm(values, gain_row):
    center = values - jnp.mean(values, axis=-1, keepdims=True)
    spread = jnp.mean(center * center, axis=-1, keepdims=True)
    return center * lax.rsqrt(spread + epsilon) * gain_row


def rotary_tables(positions, head_size):
    half_dim = head_size // 2
    exponent = jnp.arange(half_dim, dtype=jnp.float32) * (2.0 / head_size)
    inverse = jnp.power(10000.0, -exponent)
    angles = positions.astype(jnp.float32)[:, None] * inverse[None, :]
    full_angles = jnp.concatenate([angles, angles], axis=-1)
    return (jnp.cos(full_angles), jnp.sin(full_angles))


def rotate(values, cosine_table, sine_table):
    half_dim = values.shape[-1] // 2
    turned = jnp.concatenate([-values[..., half_dim:], values[..., :half_dim]], axis=-1)
    return values * cosine_table[:, None, :] + turned * sine_table[:, None, :]


def gated(gate_in, upward):
    return jax.nn.gelu(gate_in, approximate=False) * upward


def per_device(
    block_input,
    gain_before,
    joint_weight,
    mixing_weight,
    gain_middle,
    expand_weight,
    reduce_weight,
    upstream,
):
    f32 = jnp.float32
    bf16 = jnp.bfloat16
    gathered = (
        lax.all_gather(gain_before, ("seq", "fsdp"), axis=0, tiled=True),
        lax.all_gather(joint_weight, ("seq", "fsdp"), axis=0, tiled=True),
        lax.all_gather(mixing_weight, ("seq", "fsdp"), axis=0, tiled=True),
        lax.all_gather(gain_middle, ("seq", "fsdp"), axis=0, tiled=True),
        lax.all_gather(expand_weight, ("seq", "fsdp"), axis=0, tiled=True),
        lax.all_gather(reduce_weight, ("seq", "fsdp"), axis=1, tiled=True),
    )
    whole_gain_a, whole_joint, whole_mixing, whole_gain_f, whole_expand, whole_reduce = gathered
    seq_len = PIECE * lax.axis_size("seq")
    position_base = lax.axis_index("seq") * PIECE
    positions = position_base + jnp.arange(PIECE, dtype=jnp.int32)
    cosine_table, sine_table = rotary_tables(positions, HEAD_DIM)
    factor = 1.0 / math.sqrt(HEAD_DIM)
    tile_rows = min(2 * REACH, PIECE)
    tile_count = PIECE // tile_rows
    tile_keys = tile_rows + 2 * REACH
    inputs = block_input.astype(f32)
    gain_attn = whole_gain_a.astype(f32)
    normed_attn = layer_norm(inputs, gain_attn).astype(bf16)
    joint_out = jnp.einsum("gtd,de->gte", normed_attn, whole_joint, preferred_element_type=f32)
    queries = joint_out[..., :D].reshape(GROUP_SEQS, PIECE, HEADS, HEAD_DIM)
    key_rows = joint_out[..., D : 2 * D].reshape(GROUP_SEQS, PIECE, HEADS, HEAD_DIM)
    query_rot = rotate(queries, cosine_table, sine_table).astype(bf16)
    key_rot = rotate(key_rows, cosine_table, sine_table).astype(bf16)
    value_low = joint_out[..., 2 * D :].astype(bf16)
    key_value = jnp.concatenate([key_rot.reshape(GROUP_SEQS, PIECE, D), value_low], axis=-1)
    padded = with_halo(key_value, (("seq", 1),), REACH)
    padded_tiles = jnp.stack(
        [
            padded[:, index * tile_rows : index * tile_rows + tile_keys]
            for index in range(tile_count)
        ],
        axis=1,
    )
    key_heads = padded_tiles[..., :D].reshape(GROUP_SEQS, tile_count, tile_keys, HEADS, HEAD_DIM)
    value_heads = padded_tiles[..., D:].reshape(GROUP_SEQS, tile_count, tile_keys, HEADS, HEAD_DIM)
    query_tiles = query_rot.reshape(GROUP_SEQS, tile_count, tile_rows, HEADS, HEAD_DIM)
    tile_start = position_base + tile_rows * jnp.arange(tile_count, dtype=jnp.int32)
    query_pos = tile_start[:, None] + jnp.arange(tile_rows, dtype=jnp.int32)[None, :]
    key_pos = tile_start[:, None] - REACH + jnp.arange(tile_keys, dtype=jnp.int32)[None, :]
    allowed = (
        (jnp.abs(query_pos[:, :, None] - key_pos[:, None, :]) <= REACH)
        & (key_pos[:, None, :] >= 0)
        & (key_pos[:, None, :] < seq_len)
    )
    allowed = allowed[:, None]

    def window_scores():
        raw_scores = (
            jnp.einsum("gbqhd,gbkhd->gbhqk", query_tiles, key_heads, preferred_element_type=f32)
            * factor
        )
        return jnp.where(allowed, raw_scores, masked_value)

    scores = window_scores()
    maxima = jnp.max(scores, axis=-1, keepdims=True)
    exponent_terms = jnp.exp(scores - maxima)
    row_totals = jnp.sum(exponent_terms, axis=-1, keepdims=True)
    probs = exponent_terms / row_totals
    log_total = maxima + jnp.log(row_totals)
    probs_low = probs.astype(bf16)
    context = jnp.einsum("gbhqk,gbkhd->gbqhd", probs_low, value_heads, preferred_element_type=f32)
    context = context.reshape(GROUP_SEQS, PIECE, D).astype(bf16)
    middle = inputs + jnp.einsum("gtd,de->gte", context, whole_mixing, preferred_element_type=f32)
    gain_ffn = whole_gain_f.astype(f32)
    normed_ffn = layer_norm(middle, gain_ffn).astype(bf16)
    expanded = jnp.einsum("gtd,de->gte", normed_ffn, whole_expand, preferred_element_type=f32)
    gate_in = expanded[..., :FF]
    upward = expanded[..., FF:]
    hidden = gated(gate_in, upward).astype(bf16)
    output_full = middle + jnp.einsum(
        "gtf,fd->gtd", hidden, whole_reduce, preferred_element_type=f32
    )
    block_output = output_full.astype(bf16)
    back_gain_a, back_joint, back_mixing, back_gain_f, back_expand, back_reduce = gathered
    reduce_grad = jnp.einsum("gtf,gtd->fd", hidden, upstream, preferred_element_type=f32)
    d_hidden = jnp.einsum("gtd,fd->gtf", upstream, back_reduce, preferred_element_type=f32)
    unused_gate, gate_pull = jax.vjp(gated, gate_in, upward)
    d_gate, d_up = gate_pull(d_hidden)
    d_expanded = jnp.concatenate([d_gate, d_up], axis=-1).astype(bf16)
    expand_grad = jnp.einsum("gtd,gte->de", normed_ffn, d_expanded, preferred_element_type=f32)
    d_normed_ffn = jnp.einsum("gte,de->gtd", d_expanded, back_expand, preferred_element_type=f32)
    unused_norm, norm_pull = jax.vjp(layer_norm, middle, back_gain_f.astype(f32))
    d_middle_norm, middle_gain_grad = norm_pull(d_normed_ffn)
    d_middle = upstream.astype(f32) + d_middle_norm
    d_mixed = d_middle.astype(bf16)
    mixing_grad = jnp.einsum("gtd,gte->de", context, d_mixed, preferred_element_type=f32)
    d_context = jnp.einsum("gte,de->gtd", d_mixed, back_mixing, preferred_element_type=f32).astype(
        bf16
    )
    d_context = d_context.reshape(GROUP_SEQS, tile_count, tile_rows, HEADS, HEAD_DIM)
    probs_again = jnp.exp(window_scores() - log_total)
    d_probs = jnp.einsum("gbqhd,gbkhd->gbhqk", d_context, value_heads, preferred_element_type=f32)
    inner_sum = jnp.sum(probs_again * d_probs, axis=-1, keepdims=True)
    d_scores = (probs_again * (d_probs - inner_sum)).astype(bf16)
    d_query_rot = (
        jnp.einsum("gbhqk,gbkhd->gbqhd", d_scores, key_heads, preferred_element_type=f32) * factor
    )
    d_query_rot = d_query_rot.reshape(GROUP_SEQS, PIECE, HEADS, HEAD_DIM)
    d_key_tiles = (
        jnp.einsum("gbhqk,gbqhd->gbkhd", d_scores, query_tiles, preferred_element_type=f32) * factor
    )
    d_value_tiles = jnp.einsum(
        "gbhqk,gbqhd->gbkhd", probs_again.astype(bf16), d_context, preferred_element_type=f32
    )
    tiles_both = jnp.concatenate(
        [
            d_key_tiles.reshape(GROUP_SEQS, tile_count, tile_keys, D),
            d_value_tiles.reshape(GROUP_SEQS, tile_count, tile_keys, D),
        ],
        axis=-1,
    )
    combined = jnp.zeros((GROUP_SEQS, PIECE + 2 * REACH, 2 * D), f32)
    for index in range(tile_count):
        combined = combined.at[:, index * tile_rows : index * tile_rows + tile_keys].add(
            tiles_both[:, index]
        )
    lower_rim = combined[:, :REACH]
    upper_rim = combined[:, PIECE + REACH :]
    from_above = passed_along(lower_rim.astype(jnp.bfloat16), "seq", -1).astype(lower_rim.dtype)
    from_below = passed_along(upper_rim.astype(jnp.bfloat16), "seq", 1).astype(upper_rim.dtype)
    own_rows = combined[:, REACH : PIECE + REACH]
    own_rows = own_rows + jnp.pad(from_above, ((0, 0), (PIECE - REACH, 0), (0, 0)))
    own_rows = own_rows + jnp.pad(from_below, ((0, 0), (0, PIECE - REACH), (0, 0)))
    d_key_rot = own_rows[..., :D].reshape(GROUP_SEQS, PIECE, HEADS, HEAD_DIM)
    d_values = own_rows[..., D:]
    d_queries = rotate(d_query_rot, cosine_table, -sine_table).reshape(GROUP_SEQS, PIECE, D)
    d_key_plain = rotate(d_key_rot, cosine_table, -sine_table).reshape(GROUP_SEQS, PIECE, D)
    d_joint = jnp.concatenate([d_queries, d_key_plain, d_values], axis=-1).astype(bf16)
    joint_grad = jnp.einsum("gtd,gte->de", normed_attn, d_joint, preferred_element_type=f32)
    d_normed_attn = jnp.einsum("gte,de->gtd", d_joint, back_joint, preferred_element_type=f32)
    unused_first, first_pull = jax.vjp(layer_norm, inputs, back_gain_a.astype(f32))
    d_input_norm, before_gain_grad = first_pull(d_normed_attn)
    input_grad = d_middle + d_input_norm
    shares = (
        lax.psum_scatter(before_gain_grad, ("seq", "fsdp"), scatter_dimension=0, tiled=True),
        lax.psum_scatter(joint_grad, ("seq", "fsdp"), scatter_dimension=0, tiled=True),
        lax.psum_scatter(mixing_grad, ("seq", "fsdp"), scatter_dimension=0, tiled=True),
        lax.psum_scatter(middle_gain_grad, ("seq", "fsdp"), scatter_dimension=0, tiled=True),
        lax.psum_scatter(expand_grad, ("seq", "fsdp"), scatter_dimension=0, tiled=True),
        lax.psum_scatter(reduce_grad, ("seq", "fsdp"), scatter_dimension=1, tiled=True),
    )
    return (
        block_output,
        input_grad,
        shares[0],
        shares[1],
        shares[2],
        shares[3],
        shares[4],
        shares[5],
    )


def solution(mesh):
    in_specs = (
        P("fsdp", "seq", None),
        P(("seq", "fsdp")),
        P(("seq", "fsdp"), None),
        P(("seq", "fsdp"), None),
        P(("seq", "fsdp")),
        P(("seq", "fsdp"), None),
        P(None, ("seq", "fsdp")),
        P("fsdp", "seq", None),
    )
    out_specs = (
        P("fsdp", "seq", None),
        P("fsdp", "seq", None),
        P(("seq", "fsdp")),
        P(("seq", "fsdp"), None),
        P(("seq", "fsdp"), None),
        P(("seq", "fsdp")),
        P(("seq", "fsdp"), None),
        P(None, ("seq", "fsdp")),
    )
    return jax.shard_map(
        per_device, mesh=mesh, in_specs=in_specs, out_specs=out_specs, check_vma=False
    )
```

profile of v0, /device:TPU:0, one launch (start us, length us, event | category | flops | bytes accessed | tf_op | source)
XLA Modules:
  0.0 848.5 jit_solution(1385079036024937031)
XLA Ops:
  13.7 42.2 %all-reduce.9 = (bf16[768]{0:T(1024)(128)(2,1)S(1)}, bf16[768]{0:T(1024)(128)(2,1)S(1)}) all-reduce(bf16[768]{0:T(1024)(128)(2,1)S(1)} %dynamic-update-slice.12, bf16[768]{0:T(1024)(128)(2,1)S(1)} %dynamic-update-slice.13), channel_id=1, replica_groups=mesh['seq'=16,'fsdp'=2] {'seq','fsdp'}, use_global_device_ids=true, to_apply=%add.3 | all-reduce | flops 1536 | bytes 6144
  80.0 10.0 %fusion.48 = f32[4,512,2304]{2,1,0:T(8,128)S(1)} fusion(bf16[768,2304]{1,0:T(8,128)(2,1)} %all-gather.5.cloned.1.call-done, bf16[4,512,768]{2,1,0:T(8,128)(2,1)S(1)} %copy-done.4, f32[768]{0:T(1024)} %convert_element_type.80, f32[4,512]{1,0:T(4,128)S(1)} %fusion.76, f32[4,512]{1,0:T(4,128)S(1)} %broadcast_multiply_fusion.4), kind=kOutput, calls=%fused_computation.108 | convolution fusion | flops 7255621632 | bytes 25578496 | tf_op jit(solution)/shard_map/gtd,de->gte/dot_general | solution.py:101
  121.7 12.0 %fusion.91 = (f32[4,512,768]{2,1,0:T(8,128)}, bf16[4,512,768]{2,1,0:T(8,128)(2,1)}) fusion(f32[4,512,2304]{2,1,0:T(8,128)} %copy-done.11, f32[4,512,768]{2,1,0:T(8,128)} %copy.60, f32[512,768]{1,0:T(8,128)} %copy.59, f32[512,768]{1,0:T(8,128)} %copy.57), kind=kLoop, calls=%fused_computation.185 | loop fusion | flops 6291456 | bytes 31457280 | tf_op jit(solution)/shard_map/slice | solution.py:102
  167.6 8.8 %fusion.38 = bf16[4,4,128,12,64]{2,1,4,3,0:T(4,128)(2,1)} fusion(f32[4,4,128,12,32]{2,1,4,3,0:T(4,128)} %concatenate.78, f32[4,4,128,12,32]{2,1,4,3,0:T(4,128)} %concatenate.77, f32[4,4,128,12,64]{2,1,4,3,0:T(4,128)} %reshape.430, f32[4,128,64]{1,0,2:T(4,128)S(1)} %get-tuple-element.96, f32[4,128,64]{1,0,2:T(4,128)S(1)} %get-tuple-element.95), kind=kLoop, calls=%fused_computation.81 | loop fusion | flops 7864320 | bytes 15990784 | tf_op jit(solution)/shard_map/convert_element_type | solution.py:104
  186.2 8.8 %copy.64 = bf16[4,4,256,768]{2,3,1,0:T(8,128)(2,1)} copy(bf16[4,4,256,768]{3,2,0,1:T(8,128)(2,1)} %get-tuple-element.72) | data formatting | bytes 12582912 | tf_op jit(solution)/shard_map/slice | solution.py:116
  195.0 8.6 %copy.61 = bf16[4,4,256,768]{2,3,1,0:T(8,128)(2,1)} copy(bf16[4,4,256,768]{3,2,0,1:T(8,128)(2,1)} %get-tuple-element.73) | data formatting | bytes 12582912 | tf_op jit(solution)/shard_map/slice | solution.py:117
  203.6 16.7 %fusion.7 = (f32[4,4,12,128]{3,2,1,0:T(8,128)S(1)}, f32[4,4,12,128,256]{4,3,2,1,0:T(8,128)}) fusion(pred[4,128,256]{2,1,0:T(8,128)(4,1)S(1)} %fusion.71, bf16[4,4,256,12,64]{2,4,3,1,0:T(8,128)(2,1)} %bitcast.124, bf16[4,4,128,12,64]{2,1,4,3,0:T(4,128)(2,1)} %fusion.38), kind=kOutput, calls=%fused_computation.21 | convolution fusion | flops 824156160 | bytes 34832384 | tf_op jit(solution)/shard_map/gbqhd,gbkhd->gbhqk/dot_general | solution.py:131
  220.3 13.4 %fusion = f32[4,4,12,128]{3,2,1,0:T(8,128)S(1)} fusion(f32[4,4,12,128]{3,2,1,0:T(8,128)S(1)} %get-tuple-element.99, f32[4,4,12,128,256]{4,3,2,1,0:T(8,128)} %get-tuple-element.100, pred[4,128,256]{2,1,0:T(8,128)(4,1)S(1)} %fusion.71), kind=kLoop, calls=%fused_computation.12 | loop fusion | flops 25141248 | bytes 25493504 | tf_op jit(solution)/shard_map/reduce_sum | solution.py:139
  235.8 9.0 %divide_convert_fusion.6 = bf16[4,4,12,128,256]{4,3,2,1,0:T(8,128)(2,1)} fusion(f32[4,4,12,128]{3,2,1,0:T(8,128)S(1)} %fusion, f32[4,4,12,128]{3,2,1,0:T(8,128)S(1)} %get-tuple-element.99, f32[4,4,12,128,256]{4,3,2,1,0:T(8,128)S(1)} %copy-done, pred[4,128,256]{2,1,0:T(8,128)(4,1)S(1)} %fusion.71), kind=kLoop, calls=%fused_computation.9.clone.clone.clone.clone.1 | loop fusion | flops 31457280 | bytes 38076416 | tf_op jit(solution)/shard_map/gbhqk,gbkhd->gbqhd/dot_general | solution.py:143
  244.8 12.7 %convert_bitcast_fusion = bf16[4,4,128,12,64]{2,4,3,1,0:T(8,128)(2,1)} fusion(bf16[4,4,256,12,64]{2,4,3,1,0:T(8,128)(2,1)} %bitcast.126, bf16[4,4,12,128,256]{4,3,2,1,0:T(8,128)(2,1)} %divide_convert_fusion.6), kind=kOutput, calls=%fused_computation.124 | convolution fusion | flops 806879232 | bytes 22020096 | tf_op jit(solution)/shard_map/gbhqk,gbkhd->gbqhd/dot_general | solution.py:143
  278.7 15.2 %fusion.45 = f32[4,512,2304]{2,1,0:T(8,128)} fusion(bf16[768,2304]{1,0:T(8,128)(2,1)} %all-gather.9.cloned.1.call-done, f32[4,512,768]{2,1,0:T(8,128)} %copy-done.12, f32[768]{0:T(1024)S(1)} %copy-done.32, f32[4,512]{1,0:T(4,128)S(1)} %fusion.77, f32[4,512]{1,0:T(4,128)S(1)} %broadcast_multiply_fusion.3), kind=kOutput, calls=%fused_computation.105 | convolution fusion | flops 7254048768 | bytes 28724224 | tf_op jit(solution)/shard_map/gtd,de->gte/dot_general | solution.py:148
  293.9 29.6 %add_convert_fusion = (bf16[4,512,1152]{2,1,0:T(8,128)(2,1)}, f32[4,512,1152]{2,1,0:T(8,128)S(1)}, f32[4,512,1152]{2,1,0:T(8,128)}) fusion(f32[4,512,2304]{2,1,0:T(8,128)} %fusion.45, bf16[4,512,768]{2,1,0:T(8,128)(2,1)S(1)} %copy-done.15, bf16[1152,768]{0,1:T(8,128)(2,1)} %all-gather.11.cloned.1.call-done), kind=kOutput, calls=%fused_computation.35 | convolution fusion | flops 3796107264 | bytes 47382528 | tf_op jit(solution)/shard_map/gtd,fd->gtf/dot_general | solution.py:158
  323.5 14.6 %multiply_convert_fusion.1 = (bf16[4,512,1152]{2,1,0:T(8,128)(2,1)}, bf16[4,512,1152]{2,1,0:T(8,128)(2,1)}) fusion(f32[4,512,1152]{2,1,0:T(8,128)} %get-tuple-element.103, f32[4,512,1152]{2,1,0:T(8,128)S(1)} %get-tuple-element.67, f32[4,512,2304]{2,1,0:T(8,128)} %fusion.45), kind=kLoop, calls=%fused_computation.34 | loop fusion | flops 14155776 | bytes 47185920 | tf_op jit(solution)/shard_map/convert.11
  338.2 14.1 %multiply_reduce_fusion.1 = (f32[768]{0:T(1024)}, f32[4,512]{1,0:T(4,128)S(1)}, f32[4,512,768]{2,1,0:T(8,128)}) fusion(f32[4,512,768]{2,1,0:T(8,128)S(1)} %copy-done.13, f32[4,512]{1,0:T(4,128)S(1)} %fusion.77, f32[4,512]{1,0:T(4,128)S(1)} %broadcast_multiply_fusion.3, f32[768]{0:T(1024)S(1)} %copy-done.32, ...), kind=kOutput, calls=%fused_computation.84 | convolution fusion | flops 7277638656 | bytes 25589760 | tf_op jit(solution)/shard_map/gte,de->gtd/dot_general | solution.py:163
  376.9 14.5 %fusion.2 = f32[4,4,12,64,256]{4,3,2,1,0:T(8,128)} fusion(f32[4,4,12,128]{3,2,1,0:T(8,128)S(1)} %log_add_fusion, f32[4,4,12,128,256]{4,3,2,1,0:T(8,128)} %get-tuple-element.100, pred[4,128,256]{2,1,0:T(8,128)(4,1)S(1)} %copy-done.7, bf16[4,4,128,12,64]{2,1,4,3,0:T(4,128)(2,1)S(1)} %reshape.433), kind=kOutput, calls=%fused_computation.15 | convolution fusion | flops 830472192 | bytes 41123840 | tf_op jit(solution)/shard_map/gbhqk,gbqhd->gbkhd/dot_general | solution.py:184
  391.4 12.8 %copy.78 = f32[4,4,256,768]{3,2,0,1:T(8,128)} copy(f32[4,4,256,768]{2,3,1,0:T(8,128)} %bitcast.129) | data formatting | bytes 25165824 | tf_op jit(solution)/shard_map/reshape | solution.py:190
  404.1 9.5 %convolution_bitcast_fusion.1 = f32[1152,768]{0,1:T(8,128)} fusion(bf16[4,512,1152]{2,1,0:T(8,128)(2,1)} %get-tuple-element.69, bf16[4,512,768]{2,1,0:T(8,128)(2,1)} %param.23), kind=kOutput, calls=%fused_computation.103 | convolution fusion | flops 3623878656 | bytes 11403264 | tf_op jit(solution)/shard_map/gtf,gtd->fd/dot_general | solution.py:157
  413.6 24.9 %multiply_reduce_fusion = (f32[4,4,12,128]{3,2,1,0:T(8,128)S(1)}, f32[4,4,12,128,256]{4,3,2,1,0:T(8,128)}) fusion(f32[4,4,12,128]{3,2,1,0:T(8,128)S(1)} %log_add_fusion, f32[4,4,12,128,256]{4,3,2,1,0:T(8,128)} %get-tuple-element.100, pred[4,128,256]{2,1,0:T(8,128)(4,1)S(1)} %copy-done.7, bf16[4,4,256,12,64]{2,4,3,1,0:T(8,128)(2,1)} %bitcast.127, ...), kind=kOutput, calls=%fused_computation.7 | convolution fusion | flops 836739072 | bytes 60096512 | tf_op jit(solution)/shard_map/gbqhd,gbkhd->gbhqk/dot_general | solution.py:174
  438.6 23.0 %multiply_convert_fusion = bf16[4,4,12,128,256]{4,3,2,1,0:T(8,128)(2,1)} fusion(f32[4,4,12,128,256]{4,3,2,1,0:T(8,128)} %get-tuple-element.106, f32[4,4,12,128]{3,2,1,0:T(8,128)S(1)} %get-tuple-element.105, f32[4,4,12,128]{3,2,1,0:T(8,128)S(1)} %log_add_fusion, f32[4,4,12,128,256]{4,3,2,1,0:T(8,128)} %get-tuple-element.100, pred[4,128,256]{2,1,0:T(8,128)(4,1)S(1)} %copy-done.7), kind=kLoop, calls=%fused_computation.6 | loop fusion | flops 37748736 | bytes 63242240 | tf_op jit(solution)/shard_map/convert_element_type | solution.py:176
  461.6 11.3 %broadcast_multiply_fusion = f32[4,4,12,64,256]{4,3,2,1,0:T(8,128)} fusion(bf16[4,4,12,128,256]{4,3,2,1,0:T(8,128)(2,1)} %multiply_convert_fusion, bf16[4,4,128,12,64]{2,1,4,3,0:T(4,128)(2,1)S(1)} %copy-done.9), kind=kOutput, calls=%fused_computation.87 | convolution fusion | flops 808452096 | bytes 28311552 | tf_op jit(solution)/shard_map/gbhqk,gbqhd->gbkhd/dot_general | solution.py:182
  472.9 12.6 %copy.77 = f32[4,4,256,768]{3,2,0,1:T(8,128)} copy(f32[4,4,256,768]{2,3,1,0:T(8,128)} %bitcast.128) | data formatting | bytes 25165824 | tf_op jit(solution)/shard_map/reshape | solution.py:189
  485.6 16.3 %fusion.41 = f32[768,2304]{1,0:T(8,128)} fusion(bf16[4,512,1152]{2,1,0:T(8,128)(2,1)} %get-tuple-element.68, bf16[4,512,1152]{2,1,0:T(8,128)(2,1)} %get-tuple-element.66, f32[4,512,768]{2,1,0:T(8,128)} %copy-done.12, f32[768]{0:T(1024)S(1)} %copy-done.33, f32[4,512]{1,0:T(4,128)S(1)} %fusion.77, f32[4,512]{1,0:T(4,128)S(1)} %broadcast_multiply_fusion.3), kind=kOutput, calls=%fused_computation.99 | convolution fusion | flops 7272923136 | bytes 22825984 | tf_op jit(solution)/shard_map/gtd,gte->de/dot_general | solution.py:162
  508.8 10.3 %scatter-add.14 = f32[4,640,1536]{2,1,0:T(8,128)} pad(f32[4,256,1536]{2,1,0:T(8,128)} %fusion.30, f32[]{:T(128)} %constant.172.clone.1), padding=0_0x0_384x0_0 | pad | bytes 22020100 | tf_op jit(solution)/shard_map/scatter-add | solution.py:196
  554.3 10.6 %multiply_bitcast_fusion.1 = (f32[4,4,128,12,64]{2,4,3,1,0:T(8,128)S(1)}, f32[4,4,12,8,8,128]{5,4,3,2,1,0:T(8,128)}) fusion(bf16[4,4,256,12,64]{2,4,3,1,0:T(8,128)(2,1)} %bitcast.125, bf16[4,4,12,128,256]{4,3,2,1,0:T(8,128)(2,1)} %multiply_convert_fusion), kind=kOutput, calls=%fused_computation.98 | convolution fusion | flops 806879232 | bytes 31457280 | tf_op jit(solution)/shard_map/gbhqk,gbkhd->gbqhd/dot_general | solution.py:178
  564.9 8.4 copy.70
  638.5 10.5 %add_convert_fusion.2 = (bf16[4,512,768]{2,1,0:T(8,128)(2,1)S(1)}, bf16[4,512,768]{2,1,0:T(8,128)(2,1)S(1)}) fusion(f32[4,512,768]{2,1,0:T(8,128)} %copy.74, f32[4,512,768]{2,1,0:T(8,128)} %copy.71, f32[512,768]{1,0:T(8,128)} %copy.73, f32[512,768]{1,0:T(8,128)} %copy.57, f32[4,512,768]{2,1,0:T(8,128)} %copy.80, f32[4,512,1536]{2,1,0:T(8,128)} %copy-done.1), kind=kLoop, calls=%fused_computation.88 | loop fusion | flops 12582912 | bytes 34603008 | tf_op jit(solution)/shard_map/convert.4
  651.7 10.6 %convolution_bitcast_fusion = f32[768,2304]{1,0:T(8,128)} fusion(bf16[4,512,768]{2,1,0:T(8,128)(2,1)S(1)} %copy-done.19, bf16[4,512,768]{2,1,0:T(8,128)(2,1)S(1)} %get-tuple-element.91, bf16[4,512,768]{2,1,0:T(8,128)(2,1)S(1)} %get-tuple-element.90, bf16[4,512,768]{2,1,0:T(8,128)(2,1)S(1)} %copy-done.5, f32[768]{0:T(1024)S(1)} %copy-done.31, ...), kind=kOutput, calls=%fused_computation.100 | convolution fusion | flops 7283933184 | bytes 19680256 | tf_op jit(solution)/shard_map/gtd,gte->de/dot_general | solution.py:211
  662.4 10.9 %add_convert_fusion.3 = bf16[4,512,768]{2,1,0:T(8,128)(2,1)} fusion(f32[4,512,768]{2,1,0:T(8,128)} %copy-done.12, bf16[4,512,1152]{2,1,0:T(8,128)(2,1)} %get-tuple-element.69, bf16[1152,768]{0,1:T(8,128)(2,1)} %all-gather.11.cloned.1.call-done), kind=kOutput, calls=%fused_computation.91 | convolution fusion | flops 3627024384 | bytes 15925248 | tf_op jit(solution)/shard_map/gtf,fd->gtd/dot_general | solution.py:152
  673.4 11.5 %fusion.24 = (f32[4,512]{1,0:T(4,128)S(1)}, f32[4,512,768]{2,1,0:T(8,128)S(1)}) fusion(bf16[4,512,768]{2,1,0:T(8,128)(2,1)S(1)} %copy-done.5, f32[768]{0:T(1024)S(1)} %copy-done.31, f32[4,512]{1,0:T(4,128)S(1)} %copy-done.24, bf16[768,2304]{1,0:T(8,128)(2,1)} %all-gather.5.cloned.1.call-done, bf16[4,512,768]{2,1,0:T(8,128)(2,1)} %slice.335, ...), kind=kOutput, calls=%fused_computation.61 | convolution fusion | flops 7283931136 | bytes 22432768 | tf_op jit(solution)/shard_map/gte,de->gtd/dot_general | solution.py:212
  690.8 42.1 %all-reduce.8 = (f32[768]{0:T(1024)S(1)}, f32[768]{0:T(1024)S(1)}) all-reduce(f32[768]{0:T(1024)S(1)} %get-tuple-element.58, f32[768]{0:T(1024)S(1)} %copy-done.34), channel_id=2, replica_groups=mesh['seq'=16,'fsdp'=2] {'seq','fsdp'}, use_global_device_ids=true, to_apply=%region_12.13.clone | all-reduce | flops 1536 | bytes 12288
  734.1 9.5 %add_add_fusion.2 = f32[4,512,768]{2,1,0:T(8,128)} fusion(f32[4,512,768]{2,1,0:T(8,128)} %copy-done.3, bf16[4,512,768]{2,1,0:T(8,128)(2,1)} %param.23, f32[4,512]{1,0:T(4,128)S(1)} %negate_multiply_fusion.1, f32[4,512]{1,0:T(4,128)S(1)} %copy-done.28, f32[4,512]{1,0:T(4,128)S(1)} %multiply_multiply_fusion.5, f32[4,512]{1,0:T(4,128)S(1)} %copy-done.24, ...), kind=kLoop, calls=%fused_computation.85 | loop fusion | flops 18874368 | bytes 25209856 | tf_op jit(solution)/shard_map/add | solution.py:215
  743.6 97.6 %reduce-scatter.7.cloned.1.call-done = f32[24,2304]{1,0:T(8,128)} async-done(((f32[768,2304]{1,0:T(8,128)}), f32[24,2304]{1,0:T(8,128)}) %reduce-scatter.7.cloned.1.call-update) | async-done | bytes 221200 | tf_op jit(solution)/shard_map/reduce_scatter | solution.py:218
  (191 shorter events, 270.6 us)
Async XLA Ops:
  7.2 72.8 %all-gather.5.cloned.1.call-start = ((), (), s32[]{:S(2)}) async-start(), calls=%async_computation.4 | async-start | bytes 3649536 | tf_op jit(solution)/shard_map/all_gather | solution.py:83
  7.9 261.9 %all-gather.7.cloned.1.call-start = ((), (), s32[]{:S(2)}) async-start(), calls=%async_computation.5 | async-start | bytes 1216512 | tf_op jit(solution)/shard_map/all_gather | solution.py:84
  8.6 270.0 %all-gather.9.cloned.1.call-start = ((), (), s32[]{:S(2)}) async-start(), calls=%async_computation.6 | async-start | bytes 3649536 | tf_op jit(solution)/shard_map/all_gather | solution.py:86
  9.4 284.5 %all-gather.11.cloned.1.call-start = ((), (), s32[]{:S(2)}) async-start(), calls=%async_computation.7 | async-start | bytes 1824768 | tf_op jit(solution)/shard_map/all_gather | solution.py:87
  10.0 733.7 %reduce-scatter.9.cloned.1.call-start = ((), (), s32[]{:S(2)}) async-start(), calls=%async_computation.9 | async-start | bytes 2433024 | tf_op jit(solution)/shard_map/reduce_scatter | solution.py:219
  59.4 20.6 %copy-start.23 = (f32[4,512]{1,0:T(4,128)}, f32[4,512]{1,0:T(4,128)S(1)}, u32[]{:S(2)}) copy-start(f32[4,512]{1,0:T(4,128)S(1)} %broadcast_multiply_fusion.4) | copy-start | bytes 24580
  62.4 17.6 %copy-start.25 = (f32[4,512]{1,0:T(4,128)}, f32[4,512]{1,0:T(4,128)S(1)}, u32[]{:S(2)}) copy-start(f32[4,512]{1,0:T(4,128)S(1)} %fusion.76) | copy-start | bytes 24580
  66.1 13.9 %copy-start.4 = (bf16[4,512,768]{2,1,0:T(8,128)(2,1)S(1)}, bf16[4,512,768]{2,1,0:T(8,128)(2,1)}, u32[]{:S(2)}) copy-start(bf16[4,512,768]{2,1,0:T(8,128)(2,1)} %param.16) | copy-start | bytes 9437188
  80.0 153.7 %copy-start.6 = (pred[4,128,256]{2,1,0:T(8,128)(4,1)}, pred[4,128,256]{2,1,0:T(8,128)(4,1)S(1)}, u32[]{:S(2)}) copy-start(pred[4,128,256]{2,1,0:T(8,128)(4,1)S(1)} %fusion.71) | copy-start | bytes 393220
  143.2 33.2 %collective-permute-start = (bf16[4,64,1536]{2,1,0:T(8,128)(2,1)}, bf16[4,64,1536]{2,1,0:T(8,128)(2,1)}, u32[]{:S(2)}, u32[]{:S(2)}) collective-permute-start(bf16[4,64,1536]{2,1,0:T(8,128)(2,1)} %get-tuple-element.86), channel_id=1, source_target_pairs={{0,2},{2,4},{4,6},{6,8},{8,10},{10,12},{12,14},{14,16},{16,18},{18... | collective-permute-start | bytes 2359304 | tf_op jit(solution)/shard_map/ppermute | solution.py:29
  145.6 30.8 %collective-permute-start.1 = (bf16[4,64,1536]{2,1,0:T(8,128)(2,1)}, bf16[4,64,1536]{2,1,0:T(8,128)(2,1)}, u32[]{:S(2)}, u32[]{:S(2)}) collective-permute-start(bf16[4,64,1536]{2,1,0:T(8,128)(2,1)} %get-tuple-element.87), channel_id=1, source_target_pairs={{2,0},{4,2},{6,4},{8,6},{10,8},{12,10},{14,12},{16,14},{18,16},{20... | collective-permute-start | bytes 2359304 | tf_op jit(solution)/shard_map/ppermute | solution.py:31
  220.3 15.5 %copy-start = (f32[4,4,12,128,256]{4,3,2,1,0:T(8,128)S(1)}, f32[4,4,12,128,256]{4,3,2,1,0:T(8,128)}, u32[]{:S(2)}) copy-start(f32[4,4,12,128,256]{4,3,2,1,0:T(8,128)} %get-tuple-element.100) | copy-start | bytes 75497472
  235.8 9.0 %copy-start.21 = (f32[4,4,12,128]{3,2,1,0:T(8,128)}, f32[4,4,12,128]{3,2,1,0:T(8,128)S(1)}, u32[]{:S(2)}) copy-start(f32[4,4,12,128]{3,2,1,0:T(8,128)S(1)} %fusion) | copy-start | bytes 294916
  278.7 15.3 %copy-start.15 = (bf16[4,512,768]{2,1,0:T(8,128)(2,1)S(1)}, bf16[4,512,768]{2,1,0:T(8,128)(2,1)}, u32[]{:S(2)}) copy-start(bf16[4,512,768]{2,1,0:T(8,128)(2,1)} %param.23) | copy-start | bytes 9437188
  323.5 14.7 %copy-start.13 = (f32[4,512,768]{2,1,0:T(8,128)S(1)}, f32[4,512,768]{2,1,0:T(8,128)}, u32[]{:S(2)}) copy-start(f32[4,512,768]{2,1,0:T(8,128)} %copy-done.12) | copy-start | bytes 18874372
  376.8 366.8 %reduce-scatter.13.cloned.1.call-start = ((), (), s32[]{:S(2)}) async-start(), calls=%async_computation.11 | async-start | bytes 3649536
  438.6 305.1 %reduce-scatter.11.cloned.1.call-start = ((), (), s32[]{:S(2)}) async-start(), calls=%async_computation.10 | async-start | bytes 7299072 | tf_op jit(solution)/shard_map/reduce_scatter | solution.py:221
  438.6 23.0 %copy-start.9 = (bf16[4,4,128,12,64]{2,1,4,3,0:T(4,128)(2,1)S(1)}, bf16[4,4,128,12,64]{2,1,4,3,0:T(4,128)(2,1)}, u32[]{:S(2)}) copy-start(bf16[4,4,128,12,64]{2,1,4,3,0:T(4,128)(2,1)} %fusion.38) | copy-start | bytes 9437188
  472.9 12.6 %copy-start.33 = (f32[768]{0:T(1024)S(1)}, f32[768]{0:T(1024)}, u32[]{:S(2)}) copy-start(f32[768]{0:T(1024)} %convert_element_type.90) | copy-start | bytes 9220
  501.8 339.3 %reduce-scatter.7.cloned.1.call-start = ((), (), s32[]{:S(2)}) async-start(), calls=%async_computation.8 | async-start | bytes 7299072 | tf_op jit(solution)/shard_map/reduce_scatter | solution.py:218
  501.9 17.2 %slice-start = ((s8[12582912]{0:T(1024)(128)(4,1)}), s8[4194304]{0:T(1024)(128)(4,1)S(1)}, s32[]{:S(2)}) async-start(s8[12582912]{0:T(1024)(128)(4,1)} %bitcast.121), calls=%async_computation.12 | async-start | bytes 8388608
  501.9 17.2 %slice-start.1 = ((s8[12582912]{0:T(1024)(128)(4,1)}), s8[4194304]{0:T(1024)(128)(4,1)S(1)}, s32[]{:S(2)}) async-start(s8[12582912]{0:T(1024)(128)(4,1)} %bitcast.121), calls=%async_computation.13 | async-start | bytes 8388608
  508.8 10.3 %slice-start.2 = ((s8[12582912]{0:T(1024)(128)(4,1)}), s8[4194304]{0:T(1024)(128)(4,1)S(1)}, s32[]{:S(2)}) async-start(s8[12582912]{0:T(1024)(128)(4,1)} %bitcast.121), calls=%async_computation.14 | async-start | bytes 8388608
  548.0 54.3 %collective-permute-start.2 = (bf16[4,64,1536]{2,1,0:T(8,128)(2,1)S(1)}, bf16[4,64,1536]{2,1,0:T(8,128)(2,1)S(1)}, u32[]{:S(2)}, u32[]{:S(2)}) collective-permute-start(bf16[4,64,1536]{2,1,0:T(8,128)(2,1)S(1)} %slice.338), channel_id=1, source_target_pairs={{2,0},{4,2},{6,4},{8,6},{10,8},{12,10},{14,12},{16,14},{18,16},{20... | collective-permute-start | bytes 2359304 | tf_op jit(solution)/shard_map/ppermute | solution.py:41
  549.3 53.0 %collective-permute-start.3 = (bf16[4,64,1536]{2,1,0:T(8,128)(2,1)S(1)}, bf16[4,64,1536]{2,1,0:T(8,128)(2,1)S(1)}, u32[]{:S(2)}, u32[]{:S(2)}) collective-permute-start(bf16[4,64,1536]{2,1,0:T(8,128)(2,1)S(1)} %slice.337), channel_id=1, source_target_pairs={{0,2},{2,4},{4,6},{6,8},{8,10},{10,12},{12,14},{14,16},{16,18},{18... | collective-permute-start | bytes 2359304 | tf_op jit(solution)/shard_map/ppermute | solution.py:41
  638.5 13.2 %copy-start.5 = (bf16[4,512,768]{2,1,0:T(8,128)(2,1)S(1)}, bf16[4,512,768]{2,1,0:T(8,128)(2,1)}, u32[]{:S(2)}) copy-start(bf16[4,512,768]{2,1,0:T(8,128)(2,1)} %param.16) | copy-start | bytes 9437188
  638.5 13.2 %copy-start.19 = (bf16[4,512,768]{2,1,0:T(8,128)(2,1)S(1)}, bf16[4,512,768]{2,1,0:T(8,128)(2,1)}, u32[]{:S(2)}) copy-start(bf16[4,512,768]{2,1,0:T(8,128)(2,1)} %slice.335) | copy-start | bytes 9437188
  638.5 13.2 %copy-start.24 = (f32[4,512]{1,0:T(4,128)S(1)}, f32[4,512]{1,0:T(4,128)}, u32[]{:S(2)}) copy-start(f32[4,512]{1,0:T(4,128)} %copy-done.23) | copy-start | bytes 24580
  638.5 13.2 %copy-start.26 = (f32[4,512]{1,0:T(4,128)S(1)}, f32[4,512]{1,0:T(4,128)}, u32[]{:S(2)}) copy-start(f32[4,512]{1,0:T(4,128)} %copy-done.25) | copy-start | bytes 24580
  638.5 13.2 %copy-start.31 = (f32[768]{0:T(1024)S(1)}, f32[768]{0:T(1024)}, u32[]{:S(2)}) copy-start(f32[768]{0:T(1024)} %convert_element_type.80) | copy-start | bytes 9220
  673.4 11.6 %copy-start.30 = (f32[4,512]{1,0:T(4,128)S(1)}, f32[4,512]{1,0:T(4,128)}, u32[]{:S(2)}) copy-start(f32[4,512]{1,0:T(4,128)} %copy-done.29) | copy-start | bytes 24580
  684.9 49.2 %copy-start.28 = (f32[4,512]{1,0:T(4,128)S(1)}, f32[4,512]{1,0:T(4,128)}, u32[]{:S(2)}) copy-start(f32[4,512]{1,0:T(4,128)} %copy-done.27) | copy-start | bytes 24580
  (18 other events, 83.7 us)
Sparse Core Ops, SparseCore 0:
  10.9 63.1 all-gather.4
  77.0 52.9 all-gather.6
  132.9 62.4 all-gather.8
  198.1 54.3 all-gather.10
  376.9 101.7 reduce-scatter.8
  485.5 105.6 reduce-scatter.12
  598.3 118.3 reduce-scatter.10
  723.0 118.1 reduce-scatter.6
where the time goes:
time: 854 us; the launch traced here: 848 us
  matrix products  233 us (27%)
  local copies, waits for them, and re-layouts  221 us (26%)
  other arithmetic  185 us (22%)
  waiting for transfers between devices  100 us (12%)
  blocking collectives  84.3 us (10%)
  between operations  15.2 us (2%)
  starting transfers between devices  10.3 us (1%)
    reduce_scatter x1, waiting for transfers between devices, per_device(): lax.psum_scatter(joint_grad, ('seq', 'fsdp'), scatter_dimension=0, tiled=...  97.6 us
    unnamed x2, blocking collectives  84.3 us
    concatenate x5, local copies, waits for them, and re-layouts, rotate(): jnp.concatenate([-values[..., half_dim:], values[..., :half_dim]], axis=-1)  29.7 us
    dot_general x1, matrix products, per_device(): jnp.einsum('gtd,fd->gtf', upstream, back_reduce, preferred_element_type=f32)  29.6 us
    unnamed x82, local copies, waits for them, and re-layouts  25.6 us
    another operation x2, other arithmetic  25.2 us
    dot_general x1, matrix products, per_device(): jnp.einsum('gbqhd,gbkhd->gbhqk', d_context, value_heads, preferred_elemen...  24.9 us
    convert_element_type x1, other arithmetic, per_device(): d_scores = (probs_again * (d_probs - inner_sum)).astype(bf16)  23 us
  transfers between devices with their start and end apart: 12, of which 1 were waited for; matrix products, arithmetic and copies ran while one was open for 63% of the time, Pallas kernels for 0%

commit v1 on v0

v1 whole, which is shorter than its diff:
```python
import math

import jax
import jax.numpy as jnp
from jax import lax
from jax.experimental import pallas as pl
from jax.experimental.pallas import tpu as pltpu
from jax.sharding import PartitionSpec as P

HEAD_DIM = 64
REACH = 64
PAIR = 2 * HEAD_DIM
TILE = 128
KEYS = TILE + 2 * REACH
AXES = ("seq", "fsdp")

epsilon = 1e-05
masked_value = -1e30
f32 = jnp.float32
bf16 = jnp.bfloat16
VMEM_LIMIT = 56 * 1024 * 1024


def call(body, grid, in_specs, out_specs, out_shape, flops, moved, scratch=()):
    return pl.pallas_call(
        body,
        grid=grid,
        in_specs=in_specs,
        out_specs=out_specs,
        out_shape=out_shape,
        scratch_shapes=list(scratch),
        compiler_params=pltpu.CompilerParams(
            vmem_limit_bytes=VMEM_LIMIT,
            dimension_semantics=("arbitrary",) * len(grid),
        ),
        cost_estimate=pl.CostEstimate(flops=flops, bytes_accessed=moved, transcendentals=0),
    )


def dot_nn(a, b):
    return lax.dot_general(a, b, (((1,), (0,)), ((), ())), preferred_element_type=f32)


def dot_nt(a, b):
    return lax.dot_general(a, b, (((1,), (1,)), ((), ())), preferred_element_type=f32)


def dot_tn(a, b):
    return lax.dot_general(a, b, (((0,), (0,)), ((), ())), preferred_element_type=f32)


def low_half(shape):
    lane = lax.broadcasted_iota(jnp.int32, shape, 1)
    return (lane % HEAD_DIM) < HEAD_DIM // 2


def spin(values, cosine, sine):
    half = HEAD_DIM // 2
    turned = jnp.where(
        low_half(values.shape),
        pltpu.roll(values, PAIR - half, 1),
        pltpu.roll(values, half, 1),
    )
    return values * cosine + turned * sine


def normalized(values):
    center = values - jnp.mean(values, axis=-1, keepdims=True)
    spread = jnp.mean(center * center, axis=-1, keepdims=True)
    inverse = lax.rsqrt(spread + epsilon)
    return center * inverse, inverse


def norm_back(e, gain, xhat, inverse):
    eg = e * gain
    return (
        eg - jnp.mean(eg, axis=-1, keepdims=True) - xhat * jnp.mean(eg * xhat, axis=-1, keepdims=True)
    ) * inverse


def joint_body(x_ref, w_ref, gain_ref, cos_ref, sin_ref, normed_ref, qkv_ref):
    width = x_ref.shape[1]
    xhat, _ = normalized(x_ref[...].astype(f32))
    normed = (xhat * gain_ref[...]).astype(bf16)
    normed_ref[...] = normed
    cosine, sine = cos_ref[...], sin_ref[...]
    step = 2 * PAIR
    for col in range(0, 3 * width, step):
        out = dot_nn(normed, w_ref[:, col : col + step])
        if col < 2 * width:
            out = jnp.concatenate(
                [spin(out[:, :PAIR], cosine, sine), spin(out[:, PAIR:], cosine, sine)], axis=1
            )
            if col < width:
                out = out * (1.0 / math.sqrt(HEAD_DIM))
        qkv_ref[:, col : col + step] = out.astype(bf16)


def stacked_heads(rows):
    lane = lax.broadcasted_iota(jnp.int32, rows.shape, 1)
    zero = jnp.zeros_like(rows)
    first = jnp.where(lane < HEAD_DIM, rows, zero)
    second = jnp.where(lane < HEAD_DIM, zero, rows)
    return jnp.concatenate([first, second], axis=0)


def merged_heads(both):
    lane = lax.broadcasted_iota(jnp.int32, (TILE, PAIR), 1)
    return jnp.where(lane < HEAD_DIM, both[:TILE], both[TILE:])


def window_probs(keys, queries, bias):
    scores = dot_nt(keys, queries) + bias
    top = jnp.max(scores, axis=0, keepdims=True)
    terms = jnp.exp(scores - top)
    return terms * (1.0 / jnp.sum(terms, axis=0, keepdims=True))


def attention_body(q_ref, k_ref, v_ref, kl_ref, vl_ref, kh_ref, vh_ref, bias_ref, out_ref):
    keys = jnp.concatenate([kl_ref[0], k_ref[0], kh_ref[0]], axis=0)
    values = jnp.concatenate([vl_ref[0], v_ref[0], vh_ref[0]], axis=0)
    for tile in range(q_ref.shape[1] // TILE):
        start = tile * TILE
        queries = stacked_heads(q_ref[0, start : start + TILE, :])
        probs = window_probs(keys[start : start + KEYS], queries, bias_ref[tile])
        both = dot_tn(probs.astype(bf16), values[start : start + KEYS])
        out_ref[0, start : start + TILE, :] = merged_heads(both).astype(bf16)


def attention_back_body(
    q_ref, k_ref, v_ref, kl_ref, vl_ref, kh_ref, vh_ref, bias_ref, dc_ref, cos_ref, sin_ref,
    dj_ref, edge_ref, low_ref, high_ref, dk_ref, dv_ref,
):
    width = dj_ref.shape[2] // 3
    rows = q_ref.shape[1]
    tiles = rows // TILE
    column = pl.program_id(1) * PAIR

    def cols(base):
        return pl.ds(pl.multiple_of(base + column, PAIR), PAIR)

    cosine, sine = cos_ref[...], -sin_ref[...]
    keys = jnp.concatenate([kl_ref[0], k_ref[0], kh_ref[0]], axis=0)
    values = jnp.concatenate([vl_ref[0], v_ref[0], vh_ref[0]], axis=0)
    for tile in range(tiles):
        start = tile * TILE
        key_part = keys[start : start + KEYS]
        queries = stacked_heads(q_ref[0, start : start + TILE, :])
        cotangents = stacked_heads(dc_ref[0, start : start + TILE, :])
        probs = window_probs(key_part, queries, bias_ref[tile])
        d_probs = dot_nt(values[start : start + KEYS], cotangents)
        inner = jnp.sum(probs * d_probs, axis=0, keepdims=True)
        d_scores = (probs * (d_probs - inner)).astype(bf16)
        d_value = dot_nn(probs.astype(bf16), cotangents)
        d_key = dot_nn(d_scores, queries)
        d_query = merged_heads(dot_tn(d_scores, key_part)) * (1.0 / math.sqrt(HEAD_DIM))
        d_query = spin(d_query, cosine[start : start + TILE], sine[start : start + TILE])
        dj_ref[0, start : start + TILE, cols(0)] = d_query.astype(bf16)
        if tile == 0:
            dk_ref[:TILE, :] = d_key[:TILE]
            dv_ref[:TILE, :] = d_value[:TILE]
        else:
            dk_ref[start : start + TILE, :] += d_key[:TILE]
            dv_ref[start : start + TILE, :] += d_value[:TILE]
        dk_ref[start + TILE : start + KEYS, :] = d_key[TILE:]
        dv_ref[start + TILE : start + KEYS, :] = d_value[TILE:]
    own = slice(REACH, REACH + rows)
    dj_ref[0, :, cols(width)] = spin(dk_ref[own, :], cosine, sine).astype(bf16)
    dj_ref[0, :, cols(2 * width)] = dv_ref[own, :].astype(bf16)
    for part, base in ((dk_ref, 0), (dv_ref, width)):
        edge_ref[0, :REACH, cols(base)] = part[REACH : 2 * REACH, :]
        edge_ref[0, REACH:, cols(base)] = part[rows : rows + REACH, :]
        low_ref[0, :, cols(base)] = part[:REACH, :].astype(bf16)
        high_ref[0, :, cols(base)] = part[rows + REACH :, :].astype(bf16)


def middle_body(
    x_ref, ctx_ref, up_ref, w_ref, gain_ref,
    out_ref, mixed_ref, dctx_ref, normed_ref, hidden_ref, dexp_ref,
):
    width = x_ref.shape[1]
    ff = hidden_ref.shape[1]
    gain = gain_ref[...]
    mixing = w_ref[:, :width]
    upstream = up_ref[...]
    middle = x_ref[...].astype(f32) + dot_nn(ctx_ref[...], mixing)
    xhat, inverse = normalized(middle)
    normed = (xhat * gain).astype(bf16)
    normed_ref[...] = normed
    step = 3 * PAIR
    total = middle
    e = jnp.zeros_like(middle)
    for col in range(0, ff, step):
        gate_w = w_ref[:, width + col : width + col + step]
        up_w = w_ref[:, width + ff + col : width + ff + col + step]
        reduce_w = w_ref[:, width + 2 * ff + col : width + 2 * ff + col + step]
        gate = dot_nn(normed, gate_w)
        upward = dot_nn(normed, up_w)
        d_hidden = dot_nn(upstream, reduce_w)
        cdf = 0.5 + 0.5 * lax.erf(gate * math.sqrt(0.5))
        slope = cdf + gate * jnp.exp(-0.5 * gate * gate) * (1.0 / math.sqrt(2.0 * math.pi))
        act = gate * cdf
        hidden = (act * upward).astype(bf16)
        d_gate = (d_hidden * upward * slope).astype(bf16)
        d_up = (d_hidden * act).astype(bf16)
        hidden_ref[:, col : col + step] = hidden
        dexp_ref[:, col : col + step] = d_gate
        dexp_ref[:, ff + col : ff + col + step] = d_up
        total = total + dot_nt(hidden, reduce_w)
        e = e + dot_nt(d_gate, gate_w) + dot_nt(d_up, up_w)
    out_ref[...] = total.astype(bf16)
    d_middle = upstream.astype(f32) + norm_back(e, gain, xhat, inverse)
    mixed = d_middle.astype(bf16)
    mixed_ref[...] = mixed
    dctx_ref[...] = dot_nt(mixed, mixing).astype(bf16)


def joint_grad_body(
    dj_ref, edge_ref, below_ref, above_ref, normed_ref, cos_ref, sin_ref, out_ref, grad_ref, acc_ref
):
    width = normed_ref.shape[2]
    rows = dj_ref.shape[1]
    out_ref[0, REACH : rows - REACH, :] = dj_ref[0, REACH : rows - REACH, :]
    for source, at, came in ((0, 0, below_ref), (REACH, rows - REACH, above_ref)):
        here = slice(at, at + REACH)
        out_ref[0, here, :width] = dj_ref[0, here, :width]
        cosine, sine = cos_ref[here, :], -sin_ref[here, :]
        for col in range(0, 2 * width, PAIR):
            piece = slice(col, col + PAIR)
            total = edge_ref[0, source : source + REACH, piece] + came[0, :, piece].astype(f32)
            if col < width:
                total = spin(total, cosine, sine)
            out_ref[0, here, width + col : width + col + PAIR] = total.astype(bf16)
    index = pl.program_id(0)

    @pl.when(index == 0)
    def _():
        acc_ref[...] = jnp.zeros_like(acc_ref)

    flipped = normed_ref[0].T
    step = 2 * PAIR
    for col in range(0, 3 * width, step):
        acc_ref[:, col : col + step] += dot_nn(flipped, out_ref[0, :, col : col + step])

    @pl.when(index == pl.num_programs(0) - 1)
    def _():
        grad_ref[...] = acc_ref[...].astype(bf16)


def weight_grad_body(
    ctx_ref, mixed_ref, normed_ref, dexp_ref, up_ref, hidden_ref, grad_ref, acc_ref
):
    index = pl.program_id(0)

    @pl.when(index == 0)
    def _():
        acc_ref[...] = jnp.zeros_like(acc_ref)

    base = 0
    step = 3 * PAIR
    for left, right in ((ctx_ref, mixed_ref), (normed_ref, dexp_ref), (up_ref, hidden_ref)):
        flipped = left[...].T
        for col in range(0, right.shape[1], step):
            acc_ref[:, base + col : base + col + step] += dot_nn(
                flipped, right[:, col : col + step]
            )
        base += right.shape[1]

    @pl.when(index == pl.num_programs(0) - 1)
    def _():
        grad_ref[...] = acc_ref[...].astype(bf16)


def input_body(dj_ref, w_ref, x_ref, mixed_ref, gain_ref, out_ref):
    e = dot_nt(dj_ref[...], w_ref[:, : dj_ref.shape[1]])
    xhat, inverse = normalized(x_ref[...].astype(f32))
    out_ref[...] = mixed_ref[...].astype(f32) + norm_back(e, gain_ref[...], xhat, inverse)


def shifted(x, by):
    devices = lax.axis_size("seq")
    pairs = [(i, i + by) for i in range(devices) if 0 <= i + by < devices]
    return lax.ppermute(x, "seq", pairs)


def per_device(
    block_input, gain_before, joint_weight, mixing_weight, gain_middle, expand_weight,
    reduce_weight, upstream,
):
    seqs, piece, width = block_input.shape
    ff = reduce_weight.shape[0]
    tokens = seqs * piece
    pairs = width // PAIR
    shard = gain_before.shape[0]
    devices = lax.axis_size("seq")

    lead = jnp.concatenate(
        [
            joint_weight,
            gain_before[:, None],
            gain_middle[:, None],
            jnp.zeros((shard, PAIR - 2), bf16),
        ],
        axis=1,
    )
    lead = lax.all_gather(lead, AXES, axis=0, tiled=True)
    rest = jnp.concatenate([mixing_weight, expand_weight, reduce_weight.T], axis=1)
    rest = lax.all_gather(rest, AXES, axis=0, tiled=True)
    gain_a = lead[:, 3 * width].astype(f32)[None, :]
    gain_f = lead[:, 3 * width + 1].astype(f32)[None, :]

    place = lax.axis_index("seq")
    positions = place * piece + jnp.arange(piece, dtype=jnp.int32)
    half = HEAD_DIM // 2
    exponent = jnp.arange(half, dtype=f32) * (2.0 / HEAD_DIM)
    inverse = jnp.power(10000.0, -exponent)
    angles = positions.astype(f32)[:, None] * inverse[None, :]
    cosine, sine = jnp.cos(angles), jnp.sin(angles)
    cosine = jnp.concatenate([cosine] * 4, axis=-1)
    sine = jnp.concatenate([-sine, sine, -sine, sine], axis=-1)

    tiles = piece // TILE
    tile = jnp.arange(tiles, dtype=jnp.int32)[:, None, None]
    key = jnp.arange(KEYS, dtype=jnp.int32)[None, :, None]
    query = jnp.arange(2 * TILE, dtype=jnp.int32)[None, None, :] % TILE
    key_pos = place * piece + tile * TILE - REACH + key
    gap = key - query
    allowed = (gap >= 0) & (gap <= 2 * REACH) & (key_pos >= 0) & (key_pos < devices * piece)
    bias = jnp.where(allowed, 0.0, masked_value).astype(f32)

    block = 256
    steps = tokens // block
    per_seq = piece // block
    x_flat = block_input.reshape(tokens, width)
    up_flat = upstream.reshape(tokens, width)

    def rows(columns):
        return pl.BlockSpec((block, columns), lambda i: (i, 0))

    def whole(*shape):
        return pl.BlockSpec(shape, lambda *i: (0,) * len(shape))

    def shape(*dims, dtype=bf16):
        return jax.ShapeDtypeStruct(dims, dtype)

    table = pl.BlockSpec((block, PAIR), lambda i: (i % per_seq, 0))
    normed, qkv = call(
        joint_body,
        (steps,),
        [rows(width), whole(*lead.shape), whole(1, width), table, table],
        [rows(width), rows(3 * width)],
        [shape(tokens, width), shape(tokens, 3 * width)],
        6 * tokens * width * width,
        tokens * width * 10 + 6 * width * width,
    )(x_flat, lead, gain_a, cosine, sine)
    qkv = qkv.reshape(seqs, piece, 3 * width)

    from_below = shifted(qkv[:, piece - REACH :, width:], 1)
    from_above = shifted(qkv[:, :REACH, width:], -1)

    def heads(height, base):
        return pl.BlockSpec((1, height, PAIR), lambda g, j: (g, 0, base + j))

    window_specs = [
        heads(piece, 0),
        heads(piece, pairs),
        heads(piece, 2 * pairs),
        heads(REACH, 0),
        heads(REACH, pairs),
        heads(REACH, 0),
        heads(REACH, pairs),
        whole(*bias.shape),
    ]
    window_args = (
        qkv, qkv, qkv, from_below, from_below, from_above, from_above, bias,
    )
    attended = 4 * tokens * KEYS * width
    context = call(
        attention_body,
        (seqs, pairs),
        window_specs,
        heads(piece, 0),
        shape(seqs, piece, width),
        attended * 4,
        tokens * width * 8,
    )(*window_args)
    ctx_flat = context.reshape(tokens, width)

    block_output, mixed, d_context, normed_ffn, hidden, d_expanded = call(
        middle_body,
        (steps,),
        [rows(width), rows(width), rows(width), whole(*rest.shape), whole(1, width)],
        [rows(width), rows(width), rows(width), rows(width), rows(ff), rows(2 * ff)],
        [
            shape(tokens, width),
            shape(tokens, width),
            shape(tokens, width),
            shape(tokens, width),
            shape(tokens, ff),
            shape(tokens, 2 * ff),
        ],
        4 * tokens * width * (width + 3 * ff),
        tokens * (14 * width + 6 * ff) + rest.size * 2,
    )(x_flat, ctx_flat, up_flat, rest, gain_f)

    def summed(partial):
        return lax.psum_scatter(
            partial, AXES, scatter_dimension=0, tiled=True
        ).astype(f32)

    def tall(columns):
        return pl.BlockSpec((piece, columns), lambda i: (i, 0))

    rest_partial = call(
        weight_grad_body,
        (seqs,),
        [tall(width), tall(width), tall(width), tall(2 * ff), tall(width), tall(ff)],
        whole(*rest.shape),
        shape(*rest.shape),
        2 * tokens * width * (width + 3 * ff),
        tokens * (8 * width + 6 * ff) + rest.size * 2,
        [pltpu.VMEM(rest.shape, f32)],
    )(ctx_flat, mixed, normed_ffn, d_expanded, up_flat, hidden)
    d_context, rest_partial = lax.optimization_barrier((d_context, rest_partial))
    rest_grad = summed(rest_partial)
    wide = pl.BlockSpec((piece, PAIR), lambda g, j: (0, 0))
    d_joint, edges, low_rim, high_rim = call(
        attention_back_body,
        (seqs, pairs),
        window_specs + [heads(piece, 0), wide, wide],
        [
            pl.BlockSpec((1, piece, 3 * width), lambda g, j: (g, 0, 0)),
            pl.BlockSpec((1, 2 * REACH, 2 * width), lambda g, j: (g, 0, 0)),
            pl.BlockSpec((1, REACH, 2 * width), lambda g, j: (g, 0, 0)),
            pl.BlockSpec((1, REACH, 2 * width), lambda g, j: (g, 0, 0)),
        ],
        [
            shape(seqs, piece, 3 * width),
            shape(seqs, 2 * REACH, 2 * width, dtype=f32),
            shape(seqs, REACH, 2 * width),
            shape(seqs, REACH, 2 * width),
        ],
        attended * 10,
        tokens * width * 16,
        [pltpu.VMEM((piece + 2 * REACH, PAIR), f32)] * 2,
    )(*window_args, d_context.reshape(seqs, piece, width), cosine, sine)
    back_above = shifted(low_rim, -1)
    back_below = shifted(high_rim, 1)

    def one_seq(height, columns):
        return pl.BlockSpec((1, height, columns), lambda g: (g, 0, 0))

    d_joint, joint_partial = call(
        joint_grad_body,
        (seqs,),
        [
            one_seq(piece, 3 * width),
            one_seq(2 * REACH, 2 * width),
            one_seq(REACH, 2 * width),
            one_seq(REACH, 2 * width),
            one_seq(piece, width),
            whole(piece, PAIR),
            whole(piece, PAIR),
        ],
        [one_seq(piece, 3 * width), whole(width, 3 * width)],
        [shape(seqs, piece, 3 * width), shape(width, 3 * width)],
        6 * tokens * width * width,
        tokens * width * 14 + 6 * width * width,
        [pltpu.VMEM((width, 3 * width), f32)],
    )(d_joint, edges, back_below, back_above, normed.reshape(seqs, piece, width), cosine, sine)
    joint_partial, rest_grad = lax.optimization_barrier((joint_partial, rest_grad))
    joint_grad = summed(joint_partial)
    mixing_grad = rest_grad[:, :width]
    expand_grad = rest_grad[:, width : width + 2 * ff]
    reduce_grad = rest_grad[:, width + 2 * ff :].T

    input_grad = call(
        input_body,
        (steps,),
        [rows(3 * width), whole(*lead.shape), rows(width), rows(width), whole(1, width)],
        rows(width),
        shape(tokens, width, dtype=f32),
        6 * tokens * width * width,
        tokens * width * 14 + 6 * width * width,
    )(d_joint.reshape(tokens, 3 * width), lead, x_flat, mixed, gain_a)

    before_grad = jnp.sum(joint_weight.astype(f32) * joint_grad, axis=1) / gain_before.astype(f32)
    middle_grad = jnp.sum(expand_weight.astype(f32) * expand_grad, axis=1) / gain_middle.astype(f32)
    return (
        block_output.reshape(seqs, piece, width),
        input_grad.reshape(seqs, piece, width),
        before_grad,
        joint_grad,
        mixing_grad,
        middle_grad,
        expand_grad,
        reduce_grad,
    )


def solution(mesh):
    token = P("fsdp", "seq", None)
    vector = P(AXES)
    matrix = P(AXES, None)
    turned = P(None, AXES)
    in_specs = (token, vector, matrix, matrix, vector, matrix, turned, token)
    out_specs = (token, token, vector, matrix, matrix, vector, matrix, turned)
    return jax.shard_map(
        per_device, mesh=mesh, in_specs=in_specs, out_specs=out_specs, check_vma=False
    )
```

time: 854 us -> 457 us (0.54)
  matrix products: 233 us -> 0 us
  local copies, waits for them, and re-layouts: 221 us -> 9.76 us
  Pallas kernels: 0 us -> 202 us
  other arithmetic: 185 us -> 11.3 us
  waiting for transfers between devices: 100 us -> 210 us
  blocking collectives: 84.3 us -> 0 us
    dot_general x18 -> x0, matrix products: 233 us -> none  [the longest x1 29.6 us: per_device(): jnp.einsum('gtd,fd->gtf', upstream, back_reduce, preferred_element_type=f32)]
    pallas_call x0 -> x7, Pallas kernels: none -> 202 us  [the longest x1 51.3 us: per_device(): call(attention_back_body, (seqs, pairs), window_specs + [heads(piece, 0),...]
    unnamed x2 -> x0, blocking collectives: 84.3 us -> none
    all_gather x4 -> x2, waiting for transfers between devices: 0.04 us -> 83.8 us  [the longest x1 60.5 us: per_device(): lead = lax.all_gather(lead, AXES, axis=0, tiled=True)]
    slice x12 -> x2, local copies, waits for them, and re-layouts: 57.1 us -> 2.12 us  [the longest x1 1.48 us: per_device(): from_above = shifted(qkv[:, :REACH, width:], -1)]
    reshape x7 -> x0, local copies, waits for them, and re-layouts: 54.7 us -> none  [the longest x3 18.1 us: per_device(): d_query_rot = d_query_rot.reshape(GROUP_SEQS, PIECE, HEADS, HEAD_DIM)]
    unnamed x9 -> x5, waiting for transfers between devices: 2.65 us -> 35.5 us
    add x8 -> x0, other arithmetic: 31.9 us -> none  [the longest x2 14.9 us: per_device(): combined.at[:, index * tile_rows:index * tile_rows + tile_keys]]
  transfers between devices with their start and end apart: 12 -> 8, of which waited for: 1 -> 6; matrix products, arithmetic and copies ran while one was open for 63% -> 3% of each run, Pallas kernels for 0% -> 28%
where the time goes in v1:
time: 457 us; the launch traced here: 456 us
  waiting for transfers between devices  210 us (46%)
  Pallas kernels  202 us (44%)
  between operations  13.9 us (3%)
  other arithmetic  11.3 us (2%)
  local copies, waits for them, and re-layouts  9.76 us (2%)
  starting transfers between devices  8.06 us (2%)
    reduce_scatter x1, waiting for transfers between devices, summed(): lax.psum_scatter(partial, AXES, scatter_dimension=0, tiled=True).astype(f32)  87.4 us
    all_gather x1, waiting for transfers between devices, per_device(): lead = lax.all_gather(lead, AXES, axis=0, tiled=True)  60.5 us
    pallas_call x1, Pallas kernels, per_device(): call(attention_back_body, (seqs, pairs), window_specs + [heads(piece, 0),...  51.3 us
    pallas_call x1, Pallas kernels, per_device(): call(middle_body, (steps,), [rows(width), rows(width), rows(width), whole...  47.6 us
    unnamed x5, waiting for transfers between devices  35.5 us
    pallas_call x1, Pallas kernels, per_device(): call(attention_body, (seqs, pairs), window_specs, heads(piece, 0), shape(...  29.1 us
    pallas_call x1, Pallas kernels, per_device(): call(weight_grad_body, (seqs,), [tall(width), tall(width), tall(width), t...  26 us
    all_gather x1, waiting for transfers between devices, per_device(): rest = lax.all_gather(rest, AXES, axis=0, tiled=True)  23.3 us
  transfers between devices with their start and end apart: 8, of which 6 were waited for; matrix products, arithmetic and copies ran while one was open for 3% of the time, Pallas kernels for 28%

profile of v1, /device:TPU:0, one launch (start us, length us, event | category | flops | bytes accessed | tf_op | source)
XLA Modules:
  0.0 455.8 jit_solution(16043087849285323874)
XLA Ops:
  7.2 0.7 copy.23
  8.0 0.7 copy.22
  8.7 1.6 concatenate.12
  10.4 1.6 pad_maximum_fusion.2
  12.2 1.0 fusion.3
  13.2 1.3 pad_maximum_fusion
  14.4 60.5 %all-gather.3.cloned.1.call-done.w_ref = bf16[768,2432]{1,0:T(8,128)(2,1)} async-done(((bf16[24,2432]{1,0:T(8,128)(2,1)}), bf16[768,2432]{1,0:T(8,128)(2,1)}) %all-gather.3.cloned.1.call-update) | async-done | bytes 3735568 | tf_op jit(solution)/shard_map/all_gather | solution.py:306
  74.9 1.4 convert_reduce_fusion
  76.9 15.2 %shard_map.143 = (bf16[2048,768]{1,0:T(8,128)(2,1)}, bf16[2048,2304]{1,0:T(8,128)(2,1)}) custom-call(bf16[2048,768]{1,0:T(8,128)(2,1)} %bitcast.28, bf16[768,2432]{1,0:T(8,128)(2,1)} %all-gather.3.cloned.1.call-done.w_ref, f32[1,768]{1,0:T(1,128)} %reshape.181.gain_ref, f32[512,128]{1,0:T(8,128)} %get-tuple-element.57.cos_ref, ...), custom_call_target="tpu_custom_call" | custom-call | flops 7247757312 | bytes 19267584 | tf_op jit(solution)/shard_map/pallas_call | solution.py:347
  92.1 1.5 fusion.6
  93.6 1.3 collective-permute-start.1
  94.9 3.1 collective-permute-start
  98.1 1.3 and_select_fusion.bias_ref
  100.0 0.9 copy-done
  100.9 0.9 copy-done.1
  101.8 29.1 %shard_map.144 = bf16[4,512,768]{2,1,0:T(8,128)(2,1)} custom-call(bf16[4,512,2304]{2,1,0:T(8,128)(2,1)} %bitcast.15, bf16[4,512,2304]{2,1,0:T(8,128)(2,1)} %bitcast.16, bf16[4,512,2304]{2,1,0:T(8,128)(2,1)} %bitcast.17, bf16[4,64,1536]{2,1,0:T(8,128)(2,1)} %copy-done.1, bf16[4,64,1536]{2,1,0:T(8,128)(2,1)} %copy-done.1, bf16[4,64,1536]{2,1,0:T(8,128)(2,1)} %copy-done, ...), custom_call_target="tpu_custom_call" | custom-call | flops 6442450944 | bytes 12582912 | tf_op jit(solution)/shard_map/pallas_call | solution.py:378
  130.9 23.3 %all-gather.5.cloned.1.call-done.w_ref = bf16[768,4224]{1,0:T(8,128)(2,1)} async-done(((bf16[24,4224]{1,0:T(8,128)(2,1)}), bf16[768,4224]{1,0:T(8,128)(2,1)}) %all-gather.5.cloned.1.call-update) | async-done | bytes 6488080 | tf_op jit(solution)/shard_map/all_gather | solution.py:308
  154.2 47.6 %shard_map.145 = (bf16[2048,768]{1,0:T(8,128)(2,1)}, bf16[2048,768]{1,0:T(8,128)(2,1)}, bf16[2048,768]{1,0:T(8,128)(2,1)}, bf16[2048,768]{1,0:T(8,128)(2,1)}, bf...) custom-call(bf16[2048,768]{1,0:T(8,128)(2,1)} %bitcast.29, bf16[2048,768]{1,0:T(8,128)(2,1)} %bitcast.21, ...), custom_call_target="tpu_custom_call" | custom-call | flops 26575110144 | bytes 42663936 | tf_op jit(solution)/shard_map/pallas_call | solution.py:389
  201.8 26.0 %shard_map.146 = bf16[768,4224]{1,0:T(8,128)(2,1)} custom-call(bf16[2048,768]{1,0:T(8,128)(2,1)} %bitcast.22, bf16[2048,768]{1,0:T(8,128)(2,1)} %get-tuple-element.29.mixed_ref, bf16[2048,768]{1,0:T(8,128)(2,1)} %get-tuple-element.30.normed_ref, bf16[2048,2304]{1,0:T(8,128)(2,1)} %get-tuple-element.31.dexp_ref, bf16[2048,768]{1,0:T(8,128)(2,1)} %bitcast.27, ...), custom_call_target="tpu_custom_call" | custom-call | flops 13287555072 | bytes 33226752 | tf_op jit(solution)/shard_map/pallas_call | solution.py:414
  227.9 51.3 %shard_map.147 = (bf16[4,512,2304]{2,1,0:T(8,128)(2,1)}, f32[4,128,1536]{2,1,0:T(8,128)}, bf16[4,64,1536]{2,1,0:T(8,128)(2,1)}, bf16[4,64,1536]{2,1,0:T(8,128)(2,1)}) custom-call(bf16[4,512,2304]{2,1,0:T(8,128)(2,1)} %bitcast.18, bf16[4,512,2304]{2,1,0:T(8,128)(2,1)} %bitcast.19, bf16[4,512,2304]{2,1,0:T(8,128)(2,1)} %bitcast.20, ...), custom_call_target="tpu_custom_call" | custom-call | flops 16106127360 | bytes 25165824 | tf_op jit(solution)/shard_map/pallas_call | solution.py:427
  279.3 2.2 collective-permute-start.2
  281.5 1.3 collective-permute-start.3
  282.8 0.8 collective-permute-done.2.below_ref
  283.6 3.0 collective-permute-done.3.above_ref
  286.6 0.9 copy-done.7
  287.5 16.6 %shard_map.148 = (bf16[4,512,2304]{2,1,0:T(8,128)(2,1)}, bf16[768,2304]{1,0:T(8,128)(2,1)}) custom-call(bf16[4,512,2304]{2,1,0:T(8,128)(2,1)} %get-tuple-element.34.dj_ref, f32[4,128,1536]{2,1,0:T(8,128)} %get-tuple-element.35.edge_ref, bf16[4,64,1536]{2,1,0:T(8,128)(2,1)} %copy-done.6, bf16[4,64,1536]{2,1,0:T(8,128)(2,1)} %copy-done.7, ...), custom_call_target="tpu_custom_call" | custom-call | flops 7247757312 | bytes 25559040 | tf_op jit(solution)/shard_map/pallas_call | solution.py:453
  304.1 35.5 %reduce-scatter.7.cloned.1.call-done = bf16[24,4224]{1,0:T(8,128)(2,1)} async-done(((bf16[768,4224]{1,0:T(8,128)(2,1)}), bf16[24,4224]{1,0:T(8,128)(2,1)}) %reduce-scatter.7.cloned.1.call-update) | async-done | bytes 202768
  339.6 1.0 convert_element_type.57
  340.6 16.4 %shard_map.149 = f32[2048,768]{1,0:T(8,128)} custom-call(bf16[2048,2304]{1,0:T(8,128)(2,1)} %bitcast.31, bf16[768,2432]{1,0:T(8,128)(2,1)} %all-gather.3.cloned.1.call-done.w_ref, bf16[2048,768]{1,0:T(8,128)(2,1)} %bitcast.30, bf16[2048,768]{1,0:T(8,128)(2,1)} %get-tuple-element.29.mixed_ref, f32[1,768]{1,0:T(1,128)} %reshape.181.gain_ref), custom_call_target="tpu_custom_call" | custom-call | flops 7247757312 | bytes 25559040 | tf_op jit(solution)/shard_map/pallas_call | solution.py:477
  357.6 0.8 multiply_reduce_fusion
  359.6 87.4 %reduce-scatter.5.cloned.1.call-done = bf16[24,2304]{1,0:T(8,128)(2,1)} async-done(((bf16[768,2304]{1,0:T(8,128)(2,1)}), bf16[24,2304]{1,0:T(8,128)(2,1)}) %reduce-scatter.5.cloned.1.call-update) | async-done | bytes 110608 | tf_op jit(solution)/shard_map/reduce_scatter | solution.py:407
  447.0 1.7 multiply_reduce_fusion.1
  (36 shorter events, 3.9 us)
Async XLA Ops:
  7.2 67.7 %all-gather.3.cloned.1.call-start = ((), (), s32[]{:S(2)}) async-start(), calls=%async_computation.2 | async-start | bytes 3852288 | tf_op jit(solution)/shard_map/all_gather | solution.py:306
  10.4 143.9 %all-gather.5.cloned.1.call-start = ((), (), s32[]{:S(2)}) async-start(), calls=%async_computation.3 | async-start | bytes 6690816 | tf_op jit(solution)/shard_map/all_gather | solution.py:308
  12.1 327.5 %reduce-scatter.7.cloned.1.call-start = ((), (), s32[]{:S(2)}) async-start(), calls=%async_computation.5 | async-start | bytes 6690816
  93.6 6.4 %collective-permute-start.1 = (bf16[4,64,1536]{2,1,0:T(8,128)(2,1)S(1)}, bf16[4,64,1536]{2,1,0:T(8,128)(2,1)S(1)}, u32[]{:S(2)}, u32[]{:S(2)}) collective-permute-start(bf16[4,64,1536]{2,1,0:T(8,128)(2,1)S(1)} %get-tuple-element.50), channel_id=1, source_target_pairs={{2,0},{4,2},{6,4},{8,6},{10,8},{12,10},{14,12},{16,14},{18,16},{20... | collective-permute-start | bytes 2359304 | tf_op jit(solution)/shard_map/ppermute | solution.py:283
  94.9 5.1 %collective-permute-start = (bf16[4,64,1536]{2,1,0:T(8,128)(2,1)S(1)}, bf16[4,64,1536]{2,1,0:T(8,128)(2,1)S(1)}, u32[]{:S(2)}, u32[]{:S(2)}) collective-permute-start(bf16[4,64,1536]{2,1,0:T(8,128)(2,1)S(1)} %get-tuple-element.51), channel_id=1, source_target_pairs={{0,2},{2,4},{4,6},{6,8},{8,10},{10,12},{12,14},{14,16},{16,18},{18... | collective-permute-start | bytes 2359304 | tf_op jit(solution)/shard_map/ppermute | solution.py:283
  100.0 0.9 copy-start
  100.9 0.9 copy-start.1
  227.9 219.1 %reduce-scatter.5.cloned.1.call-start = ((), (), s32[]{:S(2)}) async-start(), calls=%async_computation.4 | async-start | bytes 3649536 | tf_op jit(solution)/shard_map/reduce_scatter | solution.py:407
  279.3 4.3 collective-permute-start.2
  281.5 5.1 %collective-permute-start.3 = (bf16[4,64,1536]{2,1,0:T(8,128)(2,1)}, bf16[4,64,1536]{2,1,0:T(8,128)(2,1)S(1)}, u32[]{:S(2)}, u32[]{:S(2)}) collective-permute-start(bf16[4,64,1536]{2,1,0:T(8,128)(2,1)} %get-tuple-element.37), channel_id=1, source_target_pairs={{2,0},{4,2},{6,4},{8,6},{10,8},{12,10},{14,12},{16,14},{18,16},{20... | collective-permute-start | bytes 2359304 | tf_op jit(solution)/shard_map/ppermute | solution.py:283
  283.6 3.0 copy-start.6
  286.6 0.9 copy-start.7
  340.6 17.1 %copy-start.2 = (bf16[24,2304]{1,0:T(8,128)(2,1)S(1)}, bf16[24,2304]{1,0:T(8,128)(2,1)}, u32[]{:S(2)}) copy-start(bf16[24,2304]{1,0:T(8,128)(2,1)} %param.13) | copy-start | bytes 331780
  340.6 17.9 %copy-start.4 = (bf16[24]{0:T(256)(128)(2,1)S(1)}, bf16[24]{0:T(256)(128)(2,1)}, u32[]{:S(2)}) copy-start(bf16[24]{0:T(256)(128)(2,1)} %param.12) | copy-start | bytes 148
  340.6 106.4 %copy-start.3 = (bf16[24,2304]{1,0:T(8,128)(2,1)S(1)}, bf16[24,2304]{1,0:T(8,128)(2,1)}, u32[]{:S(2)}) copy-start(bf16[24,2304]{1,0:T(8,128)(2,1)} %param.10) | copy-start | bytes 331780
  340.6 108.1 %copy-start.5 = (bf16[24]{0:T(256)(128)(2,1)S(1)}, bf16[24]{0:T(256)(128)(2,1)}, u32[]{:S(2)}) copy-start(bf16[24]{0:T(256)(128)(2,1)} %param.9) | copy-start | bytes 148
Sparse Core Ops, SparseCore 0:
  11.4 63.4 all-gather.2
  78.4 75.7 all-gather.4
  228.0 111.5 reduce-scatter.6
  344.9 102.1 reduce-scatter.4

commit v2 on v1

--- a/solution.py
+++ b/solution.py
@@ -283,6 +283,49 @@
     return lax.ppermute(x, "seq", pairs)
 
 
+def swap_order():
+    seq = [("seq", b) for b in reversed(range(lax.axis_size("seq").bit_length() - 1))]
+    fsdp = [("fsdp", b) for b in reversed(range(lax.axis_size("fsdp").bit_length() - 1))]
+    return seq + fsdp, [seq[-1]] + fsdp[::-1] + seq[-2::-1]
+
+
+def swapped(x, axis, bit):
+    return lax.ppermute(x, axis, [(i, i ^ (1 << bit)) for i in range(lax.axis_size(axis))])
+
+
+def scattered_sum(partial, earlier):
+    left, order = swap_order()
+    rows = partial.shape[0] >> len(left)
+    part = partial.reshape((2,) * len(left) + (rows, partial.shape[1]))
+    for axis, bit in order:
+        dim = left.index((axis, bit))
+        left.remove((axis, bit))
+        mine = (lax.axis_index(axis) >> bit) & 1
+        zero = lax.index_in_dim(part, 0, dim, keepdims=False)
+        one = lax.index_in_dim(part, 1, dim, keepdims=False)
+        kept = jnp.where(mine == 0, zero, one).astype(f32)
+        sent = jnp.where(mine == 0, one, zero).astype(bf16)
+        part = kept + swapped(sent, axis, bit).astype(f32)
+        if (axis, bit) == order[0]:
+            part, earlier = lax.optimization_barrier((part, earlier))
+    return part, earlier
+
+
+def gathered_rows(shard):
+    ranked, order = swap_order()
+    done = []
+    part = shard
+    for axis, bit in order[::-1]:
+        mine = (lax.axis_index(axis) >> bit) & 1
+        other = swapped(part, axis, bit)
+        zero = jnp.where(mine == 0, part, other)
+        one = jnp.where(mine == 0, other, part)
+        rank = ranked.index((axis, bit))
+        part = jnp.stack([zero, one], axis=sum(r < rank for r in done))
+        done.append(rank)
+    return part.reshape(-1, shard.shape[1])
+
+
 def per_device(
     block_input, gain_before, joint_weight, mixing_weight, gain_middle, expand_weight,
     reduce_weight, upstream,
@@ -303,7 +346,7 @@
         ],
         axis=1,
     )
-    lead = lax.all_gather(lead, AXES, axis=0, tiled=True)
+    lead = gathered_rows(lead)
     rest = jnp.concatenate([mixing_weight, expand_weight, reduce_weight.T], axis=1)
     rest = lax.all_gather(rest, AXES, axis=0, tiled=True)
     gain_a = lead[:, 3 * width].astype(f32)[None, :]
@@ -468,8 +511,7 @@
         tokens * width * 14 + 6 * width * width,
         [pltpu.VMEM((width, 3 * width), f32)],
     )(d_joint, edges, back_below, back_above, normed.reshape(seqs, piece, width), cosine, sine)
-    joint_partial, rest_grad = lax.optimization_barrier((joint_partial, rest_grad))
-    joint_grad = summed(joint_partial)
+    joint_grad, rest_grad = scattered_sum(joint_partial, rest_grad)
     mixing_grad = rest_grad[:, :width]
     expand_grad = rest_grad[:, width : width + 2 * ff]
     reduce_grad = rest_grad[:, width + 2 * ff :].T

time: 457 us -> 399 us (0.87)
  waiting for transfers between devices: 210 us -> 96.4 us
  starting transfers between devices: 8.06 us -> 56 us
  other arithmetic: 11.3 us -> 16.2 us
    reduce_scatter x1 -> x0, waiting for transfers between devices: 87.4 us -> none  [summed(): lax.psum_scatter(partial, AXES, scatter_dimension=0, tiled=True).astype(f32)]
    ppermute x0 -> x10, waiting for transfers between devices: none -> 68.5 us  [swapped(): lax.ppermute(x, axis, [(i, i ^ 1 << bit) for i in range(lax.axis_size(axi...]
    all_gather x1 -> x0, waiting for transfers between devices: 60.5 us -> none  [per_device(): lead = lax.all_gather(lead, AXES, axis=0, tiled=True)]
    ppermute x0 -> x10, starting transfers between devices: none -> 32.6 us  [swapped(): lax.ppermute(x, axis, [(i, i ^ 1 << bit) for i in range(lax.axis_size(axi...]
    all_gather x1, waiting for transfers between devices: 23.3 us -> 0.01 us  [per_device(): rest = lax.all_gather(rest, AXES, axis=0, tiled=True)]
    ppermute x4, starting transfers between devices: 7.89 us -> 23.3 us  [shifted(): return lax.ppermute(x, 'seq', pairs)]
    unnamed x5 -> x3, waiting for transfers between devices: 35.5 us -> 23.1 us
    another operation x0 -> x10, other arithmetic: none -> 5.44 us  [gathered_rows(): part = jnp.stack([zero, one], axis=sum((r < rank for r in done)))]
  transfers between devices with their start and end apart: 8 -> 16, of which waited for: 6 -> 13; matrix products, arithmetic and copies ran while one was open for 3% -> 5% of each run, Pallas kernels for 28% -> 32%
where the time goes in v2:
time: 399 us; the launch traced here: 398 us
  Pallas kernels  202 us (51%)
  waiting for transfers between devices  96.4 us (24%)
  starting transfers between devices  56 us (14%)
  other arithmetic  16.2 us (4%)
  between operations  14.3 us (4%)
  local copies, waits for them, and re-layouts  12.6 us (3%)
    ppermute x10, waiting for transfers between devices, swapped(): lax.ppermute(x, axis, [(i, i ^ 1 << bit) for i in range(lax.axis_size(axi...  68.5 us
    pallas_call x1, Pallas kernels, per_device(): call(attention_back_body, (seqs, pairs), window_specs + [heads(piece, 0),...  51.2 us
    pallas_call x1, Pallas kernels, per_device(): call(middle_body, (steps,), [rows(width), rows(width), rows(width), whole...  47.6 us
    ppermute x10, starting transfers between devices, swapped(): lax.ppermute(x, axis, [(i, i ^ 1 << bit) for i in range(lax.axis_size(axi...  32.6 us
    pallas_call x1, Pallas kernels, per_device(): call(attention_body, (seqs, pairs), window_specs, heads(piece, 0), shape(...  29.1 us
    pallas_call x1, Pallas kernels, per_device(): call(weight_grad_body, (seqs,), [tall(width), tall(width), tall(width), t...  26.1 us
    ppermute x4, starting transfers between devices, shifted(): return lax.ppermute(x, 'seq', pairs)  23.3 us
    unnamed x3, waiting for transfers between devices  23.1 us
  transfers between devices with their start and end apart: 16, of which 13 were waited for; matrix products, arithmetic and copies ran while one was open for 5% of the time, Pallas kernels for 32%

profile of v2, /device:TPU:0, one launch (start us, length us, event | category | flops | bytes accessed | tf_op | source)
XLA Modules:
  0.0 397.6 jit_solution(14162226128518864271)
XLA Ops:
  7.2 1.6 pad_maximum_fusion.7
  11.4 4.1 %collective-permute-start = (bf16[24,2432]{1,0:T(8,128)(2,1)S(1)}, bf16[24,2432]{1,0:T(8,128)(2,1)S(1)}, u32[]{:S(2)}, u32[]{:S(2)}) collective-permute-start(bf16[24,2432]{1,0:T(8,128)(2,1)S(1)} %concatenate.12), channel_id=1, source_target_pairs={{0,16},{2,18},{4,20},{6,22},{8,24},{10,26},{12,28},{14,30},{16,0},... | collective-permute-start | bytes 350216 | tf_op jit(solution)/shard_map/ppermute | solution.py:293
  15.5 5.7 %collective-permute-done = bf16[24,2432]{1,0:T(8,128)(2,1)S(1)} collective-permute-done((bf16[24,2432]{1,0:T(8,128)(2,1)S(1)}, bf16[24,2432]{1,0:T(8,128)(2,1)S(1)}, u32[]{:S(2)}, u32[]{:S(2)}) %collective-permute-start) | collective-permute-done | bytes 116768 | tf_op jit(solution)/shard_map/ppermute | solution.py:293
  22.0 8.0 %collective-permute-done.1 = bf16[2,24,2432]{2,1,0:T(8,128)(2,1)S(1)} collective-permute-done((bf16[2,24,2432]{2,1,0:T(8,128)(2,1)S(1)}, bf16[2,24,2432]{2,1,0:T(8,128)(2,1)S(1)}, u32[]{:S(2)}, u32[]{:S(2)}) %collective-permute-start.1) | collective-permute-done | bytes 233504 | tf_op jit(solution)/shard_map/ppermute | solution.py:293
  30.2 1.6 collective-permute-start.2
  31.7 9.1 %collective-permute-done.2 = bf16[2,2,24,2432]{3,2,0,1:T(8,128)(2,1)S(1)} collective-permute-done((bf16[2,2,24,2432]{3,2,0,1:T(8,128)(2,1)S(1)}, bf16[2,2,24,2432]{3,2,0,1:T(8,128)(2,1)S(1)}, u32[]{:S(2)}, u32[]{:S(2)}) %collective-permute-start.2) | collective-permute-done | bytes 466976 | tf_op jit(solution)/shard_map/ppermute | solution.py:293
  41.1 1.6 collective-permute-start.3
  42.7 21.2 %collective-permute-done.3 = bf16[2,2,2,24,2432]{4,3,0,1,2:T(8,128)(2,1)} collective-permute-done((bf16[2,2,2,24,2432]{4,3,0,1,2:T(8,128)(2,1)S(1)}, bf16[2,2,2,24,2432]{4,3,0,1,2:T(8,128)(2,1)}, u32[]{:S(2)}, u32[]{:S(2)}) %collective-permute-start.3) | collective-permute-done | bytes 933920 | tf_op jit(solution)/shard_map/ppermute | solution.py:293
  65.3 1.4 pad_maximum_fusion.1
  69.0 1.9 collective-permute-done.4
  70.9 1.9 select_bitcast_fusion.1
  75.3 15.2 %shard_map.143 = (bf16[2048,768]{1,0:T(8,128)(2,1)}, bf16[2048,2304]{1,0:T(8,128)(2,1)}) custom-call(bf16[2048,768]{1,0:T(8,128)(2,1)} %bitcast.76, bf16[768,2432]{1,0:T(8,128)(2,1)} %bitcast.66, f32[1,768]{1,0:T(1,128)} %reshape.215.gain_ref, f32[512,128]{1,0:T(8,128)} %get-tuple-element.69.cos_ref, f32[512,128]{1,0:T(8,128)} %get-tuple-element.70.sin_ref), custom_call_target="tpu_custom_call" | custom-call | flops 7247757312 | bytes 19267584 | tf_op jit(solution)/shard_map/pallas_call | solution.py:390
  90.5 1.5 fusion.10
  93.3 3.1 collective-permute-start.5
  100.2 29.1 %shard_map.144 = bf16[4,512,768]{2,1,0:T(8,128)(2,1)} custom-call(bf16[4,512,2304]{2,1,0:T(8,128)(2,1)} %bitcast.59, bf16[4,512,2304]{2,1,0:T(8,128)(2,1)} %bitcast.60, bf16[4,512,2304]{2,1,0:T(8,128)(2,1)} %bitcast.61, bf16[4,64,1536]{2,1,0:T(8,128)(2,1)} %copy-done.2, bf16[4,64,1536]{2,1,0:T(8,128)(2,1)} %copy-done.2, bf16[4,64,1536]{2,1,0:T(8,128)(2,1)} %copy-done.1, ...), custom_call_target="tpu_custom_call" | custom-call | flops 6442450944 | bytes 12582912 | tf_op jit(solution)/shard_map/pallas_call | solution.py:421
  129.3 47.6 %shard_map.145 = (bf16[2048,768]{1,0:T(8,128)(2,1)}, bf16[2048,768]{1,0:T(8,128)(2,1)}, bf16[2048,768]{1,0:T(8,128)(2,1)}, bf16[2048,768]{1,0:T(8,128)(2,1)}, bf...) custom-call(bf16[2048,768]{1,0:T(8,128)(2,1)} %bitcast.77, bf16[2048,768]{1,0:T(8,128)(2,1)} %bitcast.69, ...), custom_call_target="tpu_custom_call" | custom-call | flops 26575110144 | bytes 42663936 | tf_op jit(solution)/shard_map/pallas_call | solution.py:432
  176.9 26.1 %shard_map.146 = bf16[768,4224]{1,0:T(8,128)(2,1)} custom-call(bf16[2048,768]{1,0:T(8,128)(2,1)} %bitcast.70, bf16[2048,768]{1,0:T(8,128)(2,1)} %get-tuple-element.29.mixed_ref, bf16[2048,768]{1,0:T(8,128)(2,1)} %get-tuple-element.30.normed_ref, bf16[2048,2304]{1,0:T(8,128)(2,1)} %get-tuple-element.31.dexp_ref, bf16[2048,768]{1,0:T(8,128)(2,1)} %bitcast.75, ...), custom_call_target="tpu_custom_call" | custom-call | flops 13287555072 | bytes 33226752 | tf_op jit(solution)/shard_map/pallas_call | solution.py:457
  203.0 51.2 %shard_map.147 = (bf16[4,512,2304]{2,1,0:T(8,128)(2,1)}, f32[4,128,1536]{2,1,0:T(8,128)}, bf16[4,64,1536]{2,1,0:T(8,128)(2,1)}, bf16[4,64,1536]{2,1,0:T(8,128)(2,1)}) custom-call(bf16[4,512,2304]{2,1,0:T(8,128)(2,1)} %bitcast.62, bf16[4,512,2304]{2,1,0:T(8,128)(2,1)} %bitcast.63, bf16[4,512,2304]{2,1,0:T(8,128)(2,1)} %bitcast.64, ...), custom_call_target="tpu_custom_call" | custom-call | flops 16106127360 | bytes 25165824 | tf_op jit(solution)/shard_map/pallas_call | solution.py:470
  254.2 17.6 %collective-permute-start.7 = (bf16[4,64,1536]{2,1,0:T(8,128)(2,1)}, bf16[4,64,1536]{2,1,0:T(8,128)(2,1)S(1)}, u32[]{:S(2)}, u32[]{:S(2)}) collective-permute-start(bf16[4,64,1536]{2,1,0:T(8,128)(2,1)} %get-tuple-element.36), channel_id=1, source_target_pairs={{0,2},{2,4},{4,6},{6,8},{8,10},{10,12},{12,14},{14,16},{16,18},{18... | collective-permute-start | bytes 2359304 | tf_op jit(solution)/shard_map/ppermute | solution.py:283
  273.9 4.0 %collective-permute-done.8.above_ref = bf16[4,64,1536]{2,1,0:T(8,128)(2,1)S(1)} collective-permute-done((bf16[4,64,1536]{2,1,0:T(8,128)(2,1)}, bf16[4,64,1536]{2,1,0:T(8,128)(2,1)S(1)}, u32[]{:S(2)}, u32[]{:S(2)}) %collective-permute-start.8) | collective-permute-done | bytes 786464 | tf_op jit(solution)/shard_map/ppermute | solution.py:283
  278.8 16.8 %shard_map.148 = (bf16[4,512,2304]{2,1,0:T(8,128)(2,1)}, bf16[768,2304]{1,0:T(8,128)(2,1)}) custom-call(bf16[4,512,2304]{2,1,0:T(8,128)(2,1)} %get-tuple-element.34.dj_ref, f32[4,128,1536]{2,1,0:T(8,128)} %get-tuple-element.35.edge_ref, bf16[4,64,1536]{2,1,0:T(8,128)(2,1)} %copy-done.7, bf16[4,64,1536]{2,1,0:T(8,128)(2,1)} %copy-done.8, ...), custom_call_target="tpu_custom_call" | custom-call | flops 7247757312 | bytes 25559040 | tf_op jit(solution)/shard_map/pallas_call | solution.py:496
  295.6 2.2 fusion.11
  298.0 19.4 %collective-permute-start.9 = (bf16[2,2,2,2,24,2304]{5,4,0,1,2,3:T(8,128)(2,1)S(1)}, bf16[2,2,2,2,24,2304]{5,4,0,1,2,3:T(8,128)(2,1)S(1)}, u32[]{:S(2)}, u32[]{:S(2)}) collective-permute-start(bf16[2,2,2,2,24,2304]{5,4,0,1,2,3:T(8,128)(2,1)S(1)} %select_bitcast_fusion.2), channel_id=1, source_target_pairs={{0,2},{2,0},{4,6},{6,4},{8,10},{10,8},{12,14},{14,12},{16,18},{18,... | collective-permute-start | bytes 5308424 | tf_op jit(solution)/shard_map/ppermute | solution.py:293
  317.4 3.3 collective-permute-done.9
  321.3 23.1 %reduce-scatter.4.cloned.1.call-done = bf16[24,4224]{1,0:T(8,128)(2,1)} async-done(((bf16[768,4224]{1,0:T(8,128)(2,1)}), bf16[24,4224]{1,0:T(8,128)(2,1)}) %reduce-scatter.4.cloned.1.call-update) | async-done | bytes 202768
  345.5 1.4 collective-permute-start.10
  347.0 16.2 %shard_map.149 = f32[2048,768]{1,0:T(8,128)} custom-call(bf16[2048,2304]{1,0:T(8,128)(2,1)} %bitcast.79, bf16[768,2432]{1,0:T(8,128)(2,1)} %bitcast.67, bf16[2048,768]{1,0:T(8,128)(2,1)} %bitcast.78, bf16[2048,768]{1,0:T(8,128)(2,1)} %get-tuple-element.29.mixed_ref, f32[1,768]{1,0:T(1,128)} %reshape.215.gain_ref), custom_call_target="tpu_custom_call" | custom-call | flops 7247757312 | bytes 25559040 | tf_op jit(solution)/shard_map/pallas_call | solution.py:519
  363.1 2.2 collective-permute-done.10
  367.7 7.4 %collective-permute-done.11 = bf16[2,2,24,2304]{3,2,0,1:T(8,128)(2,1)S(1)} collective-permute-done((bf16[2,2,24,2304]{3,2,0,1:T(8,128)(2,1)S(1)}, bf16[2,2,24,2304]{3,2,0,1:T(8,128)(2,1)S(1)}, u32[]{:S(2)}, u32[]{:S(2)}) %collective-permute-start.11) | collective-permute-done | bytes 442400 | tf_op jit(solution)/shard_map/ppermute | solution.py:293
  376.9 5.5 %collective-permute-done.12 = bf16[2,24,2304]{2,1,0:T(8,128)(2,1)S(1)} collective-permute-done((bf16[2,24,2304]{2,1,0:T(8,128)(2,1)S(1)}, bf16[2,24,2304]{2,1,0:T(8,128)(2,1)S(1)}, u32[]{:S(2)}, u32[]{:S(2)}) %collective-permute-start.12) | collective-permute-done | bytes 221216 | tf_op jit(solution)/shard_map/ppermute | solution.py:293
  382.5 1.6 collective-permute-start.13
  385.3 4.1 %collective-permute-done.13 = bf16[24,2304]{1,0:T(8,128)(2,1)S(1)} collective-permute-done((bf16[24,2304]{1,0:T(8,128)(2,1)S(1)}, bf16[24,2304]{1,0:T(8,128)(2,1)S(1)}, u32[]{:S(2)}, u32[]{:S(2)}) %collective-permute-start.13) | collective-permute-done | bytes 110624 | tf_op jit(solution)/shard_map/ppermute | solution.py:293
  (73 shorter events, 26.5 us)
Async XLA Ops:
  7.2 122.1 %all-gather.2.cloned.1.call-start = ((), (), s32[]{:S(2)}) async-start(), calls=%async_computation.1 | async-start | bytes 6690816 | tf_op jit(solution)/shard_map/all_gather | solution.py:351
  8.9 335.5 %reduce-scatter.4.cloned.1.call-start = ((), (), s32[]{:S(2)}) async-start(), calls=%async_computation.2 | async-start | bytes 6690816
  11.4 9.8 %collective-permute-start = (bf16[24,2432]{1,0:T(8,128)(2,1)S(1)}, bf16[24,2432]{1,0:T(8,128)(2,1)S(1)}, u32[]{:S(2)}, u32[]{:S(2)}) collective-permute-start(bf16[24,2432]{1,0:T(8,128)(2,1)S(1)} %concatenate.12), channel_id=1, source_target_pairs={{0,16},{2,18},{4,20},{6,22},{8,24},{10,26},{12,28},{14,30},{16,0},... | collective-permute-start | bytes 350216 | tf_op jit(solution)/shard_map/ppermute | solution.py:293
  21.3 8.8 %collective-permute-start.1 = (bf16[2,24,2432]{2,1,0:T(8,128)(2,1)S(1)}, bf16[2,24,2432]{2,1,0:T(8,128)(2,1)S(1)}, u32[]{:S(2)}, u32[]{:S(2)}) collective-permute-start(bf16[2,24,2432]{2,1,0:T(8,128)(2,1)S(1)} %pad_maximum_fusion.6), channel_id=1, source_target_pairs={{0,8},{2,10},{4,12},{6,14},{8,0},{10,2},{12,4},{14,6},{16,24},{18,... | collective-permute-start | bytes 700424 | tf_op jit(solution)/shard_map/ppermute | solution.py:293
  30.2 10.7 %collective-permute-start.2 = (bf16[2,2,24,2432]{3,2,0,1:T(8,128)(2,1)S(1)}, bf16[2,2,24,2432]{3,2,0,1:T(8,128)(2,1)S(1)}, u32[]{:S(2)}, u32[]{:S(2)}) collective-permute-start(bf16[2,2,24,2432]{3,2,0,1:T(8,128)(2,1)S(1)} %pad_maximum_fusion.3), channel_id=1, source_target_pairs={{0,4},{2,6},{4,0},{6,2},{8,12},{10,14},{12,8},{14,10},{16,20},{18,... | collective-permute-start | bytes 1400840 | tf_op jit(solution)/shard_map/ppermute | solution.py:293
  41.1 22.8 %collective-permute-start.3 = (bf16[2,2,2,24,2432]{4,3,0,1,2:T(8,128)(2,1)S(1)}, bf16[2,2,2,24,2432]{4,3,0,1,2:T(8,128)(2,1)}, u32[]{:S(2)}, u32[]{:S(2)}) collective-permute-start(bf16[2,2,2,24,2432]{4,3,0,1,2:T(8,128)(2,1)S(1)} %pad_maximum_fusion.2), channel_id=1, source_target_pairs={{0,1},{1,0},{2,3},{3,2},{4,5},{5,4},{6,7},{7,6},{8,9},{9,8},{10,11... | collective-permute-start | bytes 2801672 | tf_op jit(solution)/shard_map/ppermute | solution.py:293
  66.7 4.2 %collective-permute-start.4 = (bf16[2,2,2,2,24,2432]{5,4,0,1,2,3:T(8,128)(2,1)}, bf16[2,2,2,2,24,2432]{5,4,0,1,2,3:T(8,128)(2,1)}, u32[]{:S(2)}, u32[]{:S(2)}) collective-permute-start(bf16[2,2,2,2,24,2432]{5,4,0,1,2,3:T(8,128)(2,1)} %pad_maximum_fusion.1), channel_id=1, source_target_pairs={{0,2},{2,0},{4,6},{6,4},{8,10},{10,8},{12,14},{14,12},{16,18},{18,... | collective-permute-start | bytes 5603336 | tf_op jit(solution)/shard_map/ppermute | solution.py:293
  73.4 1.8 copy-start
  92.0 6.4 %collective-permute-start.6 = (bf16[4,64,1536]{2,1,0:T(8,128)(2,1)S(1)}, bf16[4,64,1536]{2,1,0:T(8,128)(2,1)S(1)}, u32[]{:S(2)}, u32[]{:S(2)}) collective-permute-start(bf16[4,64,1536]{2,1,0:T(8,128)(2,1)S(1)} %get-tuple-element.50), channel_id=1, source_target_pairs={{2,0},{4,2},{6,4},{8,6},{10,8},{12,10},{14,12},{16,14},{18,16},{20... | collective-permute-start | bytes 2359304 | tf_op jit(solution)/shard_map/ppermute | solution.py:283
  93.3 5.1 %collective-permute-start.5 = (bf16[4,64,1536]{2,1,0:T(8,128)(2,1)S(1)}, bf16[4,64,1536]{2,1,0:T(8,128)(2,1)S(1)}, u32[]{:S(2)}, u32[]{:S(2)}) collective-permute-start(bf16[4,64,1536]{2,1,0:T(8,128)(2,1)S(1)} %get-tuple-element.51), channel_id=1, source_target_pairs={{0,2},{2,4},{4,6},{6,8},{8,10},{10,12},{12,14},{14,16},{16,18},{18... | collective-permute-start | bytes 2359304 | tf_op jit(solution)/shard_map/ppermute | solution.py:283
  98.4 0.9 copy-start.1
  99.3 0.9 copy-start.2
  254.2 19.7 %collective-permute-start.7 = (bf16[4,64,1536]{2,1,0:T(8,128)(2,1)}, bf16[4,64,1536]{2,1,0:T(8,128)(2,1)S(1)}, u32[]{:S(2)}, u32[]{:S(2)}) collective-permute-start(bf16[4,64,1536]{2,1,0:T(8,128)(2,1)} %get-tuple-element.36), channel_id=1, source_target_pairs={{0,2},{2,4},{4,6},{6,8},{8,10},{10,12},{12,14},{14,16},{16,18},{18... | collective-permute-start | bytes 2359304 | tf_op jit(solution)/shard_map/ppermute | solution.py:283
  271.9 6.0 %collective-permute-start.8 = (bf16[4,64,1536]{2,1,0:T(8,128)(2,1)}, bf16[4,64,1536]{2,1,0:T(8,128)(2,1)S(1)}, u32[]{:S(2)}, u32[]{:S(2)}) collective-permute-start(bf16[4,64,1536]{2,1,0:T(8,128)(2,1)} %get-tuple-element.37), channel_id=1, source_target_pairs={{2,0},{4,2},{6,4},{8,6},{10,8},{12,10},{14,12},{16,14},{18,16},{20... | collective-permute-start | bytes 2359304 | tf_op jit(solution)/shard_map/ppermute | solution.py:283
  273.9 4.0 %copy-start.7 = (bf16[4,64,1536]{2,1,0:T(8,128)(2,1)}, bf16[4,64,1536]{2,1,0:T(8,128)(2,1)S(1)}, u32[]{:S(2)}) copy-start(bf16[4,64,1536]{2,1,0:T(8,128)(2,1)S(1)} %collective-permute-done.7.below_ref) | copy-start | bytes 2359300
  277.9 0.9 copy-start.8
  298.0 22.7 %collective-permute-start.9 = (bf16[2,2,2,2,24,2304]{5,4,0,1,2,3:T(8,128)(2,1)S(1)}, bf16[2,2,2,2,24,2304]{5,4,0,1,2,3:T(8,128)(2,1)S(1)}, u32[]{:S(2)}, u32[]{:S(2)}) collective-permute-start(bf16[2,2,2,2,24,2304]{5,4,0,1,2,3:T(8,128)(2,1)S(1)} %select_bitcast_fusion.2), channel_id=1, source_target_pairs={{0,2},{2,0},{4,6},{6,4},{8,10},{10,8},{12,14},{14,12},{16,18},{18,... | collective-permute-start | bytes 5308424 | tf_op jit(solution)/shard_map/ppermute | solution.py:293
  345.5 19.8 %collective-permute-start.10 = (bf16[2,2,2,24,2304]{4,3,0,1,2:T(8,128)(2,1)S(1)}, bf16[2,2,2,24,2304]{4,3,0,1,2:T(8,128)(2,1)S(1)}, u32[]{:S(2)}, u32[]{:S(2)}) collective-permute-start(bf16[2,2,2,24,2304]{4,3,0,1,2:T(8,128)(2,1)S(1)} %fusion), channel_id=1, source_target_pairs={{0,1},{1,0},{2,3},{3,2},{4,5},{5,4},{6,7},{7,6},{8,9},{9,8},{10,11... | collective-permute-start | bytes 2654216 | tf_op jit(solution)/shard_map/ppermute | solution.py:293
  365.7 9.4 %collective-permute-start.11 = (bf16[2,2,24,2304]{3,2,0,1:T(8,128)(2,1)S(1)}, bf16[2,2,24,2304]{3,2,0,1:T(8,128)(2,1)S(1)}, u32[]{:S(2)}, u32[]{:S(2)}) collective-permute-start(bf16[2,2,24,2304]{3,2,0,1:T(8,128)(2,1)S(1)} %fusion.1), channel_id=1, source_target_pairs={{0,4},{2,6},{4,0},{6,2},{8,12},{10,14},{12,8},{14,10},{16,20},{18,... | collective-permute-start | bytes 1327112 | tf_op jit(solution)/shard_map/ppermute | solution.py:293
  367.7 8.4 %copy-start.3 = (bf16[24,2304]{1,0:T(8,128)(2,1)S(1)}, bf16[24,2304]{1,0:T(8,128)(2,1)}, u32[]{:S(2)}) copy-start(bf16[24,2304]{1,0:T(8,128)(2,1)} %param.13) | copy-start | bytes 331780
  375.3 8.9 %copy-start.5 = (bf16[24]{0:T(256)(128)(2,1)S(1)}, bf16[24]{0:T(256)(128)(2,1)}, u32[]{:S(2)}) copy-start(bf16[24]{0:T(256)(128)(2,1)} %param.12) | copy-start | bytes 148
  375.3 14.2 %copy-start.4 = (bf16[24,2304]{1,0:T(8,128)(2,1)S(1)}, bf16[24,2304]{1,0:T(8,128)(2,1)}, u32[]{:S(2)}) copy-start(bf16[24,2304]{1,0:T(8,128)(2,1)} %param.10) | copy-start | bytes 331780
  375.3 14.9 %copy-start.6 = (bf16[24]{0:T(256)(128)(2,1)S(1)}, bf16[24]{0:T(256)(128)(2,1)}, u32[]{:S(2)}) copy-start(bf16[24]{0:T(256)(128)(2,1)} %param.9) | copy-start | bytes 148
  375.3 7.1 %collective-permute-start.12 = (bf16[2,24,2304]{2,1,0:T(8,128)(2,1)S(1)}, bf16[2,24,2304]{2,1,0:T(8,128)(2,1)S(1)}, u32[]{:S(2)}, u32[]{:S(2)}) collective-permute-start(bf16[2,24,2304]{2,1,0:T(8,128)(2,1)S(1)} %fusion.5), channel_id=1, source_target_pairs={{0,8},{2,10},{4,12},{6,14},{8,0},{10,2},{12,4},{14,6},{16,24},{18,... | collective-permute-start | bytes 663560 | tf_op jit(solution)/shard_map/ppermute | solution.py:293
  382.5 6.9 %collective-permute-start.13 = (bf16[24,2304]{1,0:T(8,128)(2,1)S(1)}, bf16[24,2304]{1,0:T(8,128)(2,1)S(1)}, u32[]{:S(2)}, u32[]{:S(2)}) collective-permute-start(bf16[24,2304]{1,0:T(8,128)(2,1)S(1)} %fusion.6), channel_id=1, source_target_pairs={{0,16},{2,18},{4,20},{6,22},{8,24},{10,26},{12,28},{14,30},{16,0},... | collective-permute-start | bytes 331784 | tf_op jit(solution)/shard_map/ppermute | solution.py:293
Sparse Core Ops, SparseCore 0:
  11.5 77.6 all-gather.1
  203.1 141.2 reduce-scatter.3
